TPU v7x, 32 devices: a whole 2x2x4 slice. The times are simulated.
32 devices in a mesh: dp: 8 (over y, x, core), hd: 4 (over z).
Axes of the slice: x: 2, y: 2, z: 4, core: 2. Of those that a mesh axis runs over, the one named last changes fastest.
Arguments:
- query_nope: bfloat16 [512, 16384], P('dp', 'hd'), may hold values from -6 to 6
- query_rope: bfloat16 [512, 8192], P('dp', 'hd')
- latent: bfloat16 [512, 512], P('dp'), may hold values from -6 to 6
- key_rope: bfloat16 [512, 64], P('dp'), may hold values from -6 to 6
- key_up: bfloat16 [512, 16384], P(None, 'hd'), may hold values from -0.25 to 0.25
- value_up: bfloat16 [512, 16384], P(None, 'hd'), may hold values from -0.25 to 0.25
- output_weight: bfloat16 [16384, 7168], P('hd', 'dp'), may hold values from -0.046875 to 0.046875
- residual: bfloat16 [512, 7168], P('dp', 'hd'), may hold values from -6 to 6
- norm_gain: float32 [7168], P('hd'), may hold values from 0.1 to 1.9
- gate_weight: bfloat16 [7168, 18432], P('hd', 'dp'), may hold values from -0.0625 to 0.0625
- up_weight: bfloat16 [7168, 18432], P('hd', 'dp'), may hold values from -0.0625 to 0.0625
- down_weight: bfloat16 [18432, 7168], P('dp', 'hd'), may hold values from -0.046875 to 0.046875
- rank_tokens: int32 [8], replicated, may hold values from 1 to 64, 256 in all
- request_ids: int32 [8, 64], P('dp'), may hold values from 0 to 3, never falling along the last dimension, each value on 1 to 32 neighbouring positions
Outputs:
- layer_out: bfloat16 [512, 7168], P('dp', 'hd')
Inputs may be any that keep to these rules, and one draw needn't show every extreme that they name: `rank_tokens`: the counts sum to 256. `request_ids`: along each rank's slots the number never falls; one request covers at most 32 slots.
All inputs are finite; a program needn't handle non-finite values.
Results may differ from a plain program's by a relative error of at most 0.0085.
Values may be sent and summed in bfloat16 or wider, within the bound.
A program may use at most 128 MiB of HBM per device.

v0:
```python
import jax
import jax.numpy as jnp
from jax import lax
from jax.sharding import PartitionSpec as P

D = 7168
NOPE = 128
ROPE = 64
VH = 128


def attend(query_nope, query_rope, latent, key_rope, key_up, value_up, request_row):
    slots = latent.shape[0]
    heads = key_up.shape[1] // NOPE
    key_nope = jnp.dot(latent, key_up, preferred_element_type=jnp.float32).astype(jnp.bfloat16)
    values = jnp.dot(latent, value_up, preferred_element_type=jnp.float32).astype(jnp.bfloat16)
    query_heads = query_nope.reshape(slots, heads, NOPE)
    rotary_heads = query_rope.reshape(slots, heads, ROPE)
    scores = jnp.einsum(
        "shd,thd->hst",
        query_heads,
        key_nope.reshape(slots, heads, NOPE),
        preferred_element_type=jnp.float32,
    )
    scores = scores + jnp.einsum(
        "shd,td->hst", rotary_heads, key_rope, preferred_element_type=jnp.float32
    )
    scores = scores * (NOPE + ROPE) ** (-0.5)
    position = jnp.arange(slots, dtype=jnp.int32)
    allowed = (request_row[:, None] == request_row[None, :]) & (
        position[None, :] <= position[:, None]
    )
    scores = jnp.where(allowed[None, :, :], scores, jnp.float32(-1e30))
    top = jnp.max(scores, axis=-1, keepdims=True)
    raised = jnp.exp(scores - top)
    weights = (raised / jnp.sum(raised, axis=-1, keepdims=True)).astype(jnp.bfloat16)
    attended = jnp.einsum(
        "hst,thd->shd",
        weights,
        values.reshape(slots, heads, VH),
        preferred_element_type=jnp.float32,
    )
    return attended.astype(jnp.bfloat16).reshape(slots, heads * VH)


def feed_forward(partial_gate, down_weight):
    width = down_weight.shape[0]
    totals = lax.psum(partial_gate, "hd")
    hidden = (jax.nn.silu(totals[:, :width]) * totals[:, width:]).astype(jnp.bfloat16)
    return jnp.dot(hidden, down_weight, preferred_element_type=jnp.float32)


def on_device(
    query_nope,
    query_rope,
    latent,
    key_rope,
    key_up,
    value_up,
    output_weight,
    residual,
    norm_gain,
    gate_weight,
    up_weight,
    down_weight,
    rank_tokens,
    request_ids,
):
    slots = latent.shape[0]
    ranks = lax.axis_size("dp")
    attended = attend(query_nope, query_rope, latent, key_rope, key_up, value_up, request_ids[0])
    partial_proj = jnp.dot(
        lax.all_gather(attended, "dp", axis=0, tiled=True),
        output_weight,
        preferred_element_type=jnp.float32,
    )
    by_token = lax.all_to_all(partial_proj, "dp", split_axis=0, concat_axis=1, tiled=True)
    projected = lax.psum_scatter(by_token, "hd", scatter_dimension=1, tiled=True)
    mixed = (residual.astype(jnp.float32) + projected).astype(jnp.bfloat16)
    widened = mixed.astype(jnp.float32)
    square_sum = lax.psum(jnp.sum(widened * widened, axis=1), "hd")
    normed = (widened * lax.rsqrt(square_sum[:, None] / D + 1e-06) * norm_gain).astype(jnp.bfloat16)
    piece = lax.all_gather(normed, "dp", axis=0, tiled=True)
    gate_part = jnp.dot(piece, gate_weight, preferred_element_type=jnp.float32)
    up_part = jnp.dot(piece, up_weight, preferred_element_type=jnp.float32)
    partial_gate = jnp.concatenate((gate_part, up_part), axis=1)
    down_rows = feed_forward(partial_gate, down_weight)
    mlp = lax.psum_scatter(down_rows, "dp", scatter_dimension=0, tiled=True)
    index = lax.axis_index("dp")
    count = jnp.sum(jnp.where(jnp.arange(ranks, dtype=jnp.int32) == index, rank_tokens, 0))
    live = jnp.arange(slots, dtype=jnp.int32) < count
    result = (widened + mlp).astype(jnp.bfloat16)
    return jnp.where(live[:, None], result, jnp.zeros_like(result))


def solution(mesh):
    in_specs = (
        P("dp", "hd"),
        P("dp", "hd"),
        P("dp", None),
        P("dp", None),
        P(None, "hd"),
        P(None, "hd"),
        P("hd", "dp"),
        P("dp", "hd"),
        P("hd"),
        P("hd", "dp"),
        P("hd", "dp"),
        P("dp", "hd"),
        P(),
        P("dp", None),
    )
    out_specs = P("dp", "hd")
    return jax.shard_map(
        on_device, mesh=mesh, in_specs=in_specs, out_specs=out_specs, check_vma=False
    )
```

profile of v0, /device:TPU:0, one launch (start us, length us, event | category | flops | bytes accessed | tf_op | source)
XLA Modules:
  0.0 583.0 jit_solution(10125103296813134916)
XLA Ops:
  6.5 0.0 copy-start
  6.5 0.0 all-gather.3.cloned.1.call-start
  6.5 1.5 reshape.75
  8.1 0.8 fusion.25
  8.9 1.4 convolution_bitcast_fusion
  10.2 0.0 copy-start.3
  10.3 3.2 fusion.10
  13.5 0.0 copy-done
  13.5 0.4 fusion.8
  13.9 0.3 fusion.30
  14.2 0.0 copy-done.2
  14.2 0.0 copy-done.3
  14.2 0.8 fusion.9
  15.0 0.4 fusion.11
  15.5 0.9 copy.49
  16.4 0.0 all-gather.3.cloned.1.call-update
  16.4 0.0 reduce-scatter.3.cloned.1.call-start
  16.5 39.5 %all-gather.3.cloned.1.call-done = bf16[512,4096]{1,0:T(8,128)(2,1)} async-done(((bf16[64,4096]{1,0:T(8,128)(2,1)}), bf16[512,4096]{1,0:T(8,128)(2,1)}) %all-gather.3.cloned.1.call-update) | async-done | bytes 4194320 | tf_op jit(solution)/shard_map/all_gather | solution.py:73
  56.0 9.8 %fusion.31 = f32[512,896]{1,0:T(8,128)S(1)} fusion(bf16[512,4096]{1,0:T(8,128)(2,1)} %all-gather.3.cloned.1.call-done, bf16[4096,896]{1,0:T(8,128)(2,1)} %param.20), kind=kOutput, calls=%fused_computation.47 | convolution fusion | flops 3758096384 | bytes 13369344 | tf_op jit(solution)/shard_map/dot_general | solution.py:72
  65.8 0.0 copy-start.4
  65.8 0.0 copy-start.5
  65.8 26.5 %all_to_all.19 = f32[8,64,896]{2,1,0:T(8,128)S(1)} all-to-all(f32[8,64,896]{2,1,0:T(8,128)S(1)} %bitcast.57), channel_id=1, replica_groups=mesh['dp'=8,'hd'=4] {'dp'}, dimensions={0} | all-to-all | bytes 3670016 | tf_op jit(solution)/shard_map/all_to_all | solution.py:77
  92.3 1.4 copy.33
  93.7 0.0 reduce-scatter.3.cloned.1.call-update
  93.7 0.0 all-gather.5.cloned.1.call-start
  93.7 38.6 %reduce-scatter.3.cloned.1.call-done = f32[64,1792]{1,0:T(8,128)} async-done(((f32[64,7168]{1,0:T(8,128)}), f32[64,1792]{1,0:T(8,128)}) %reduce-scatter.3.cloned.1.call-update) | async-done | bytes 458768 | tf_op jit(solution)/shard_map/reduce_scatter | solution.py:78
  132.4 0.0 copy-done.4
  132.4 1.2 fusion.20
  133.6 10.0 %psum.14 = f32[64]{0:T(128)S(1)} all-reduce(f32[64]{0:T(128)S(1)} %get-tuple-element.5), channel_id=1, replica_groups=mesh['dp'=8,'hd'=4] {'hd'}, use_global_device_ids=true, to_apply=%region_5.6 | all-reduce | flops 64 | bytes 512 | tf_op jit(solution)/shard_map/psum | solution.py:81
  143.6 0.0 copy-done.5
  143.6 0.8 fusion.22
  144.4 0.0 all-gather.5.cloned.1.call-update
  144.4 0.0 all-reduce.2.cloned.1.call-start
  144.5 24.8 %all-gather.5.cloned.1.call-done = bf16[512,1792]{1,0:T(8,128)(2,1)} async-done(((bf16[64,1792]{1,0:T(8,128)(2,1)}), bf16[512,1792]{1,0:T(8,128)(2,1)}) %all-gather.5.cloned.1.call-update) | async-done | bytes 1835024 | tf_op jit(solution)/shard_map/all_gather | solution.py:83
  169.4 7.9 %fusion.32 = f32[512,2304]{1,0:T(8,128)S(1)} fusion(bf16[512,1792]{1,0:T(8,128)(2,1)} %all-gather.5.cloned.1.call-done, bf16[1792,2304]{1,0:T(8,128)(2,1)} %param.23), kind=kOutput, calls=%fused_computation.48 | convolution fusion | flops 4227858432 | bytes 14811136 | tf_op jit(solution)/shard_map/dot_general | solution.py:84
  177.3 0.0 copy-done.6
  177.3 6.8 %fusion.33 = f32[512,2304]{1,0:T(8,128)S(1)} fusion(bf16[512,1792]{1,0:T(8,128)(2,1)S(1)} %copy-done.6, bf16[1792,2304]{1,0:T(8,128)(2,1)} %param.24), kind=kOutput, calls=%fused_computation.49 | convolution fusion | flops 4227858432 | bytes 14811136 | tf_op jit(solution)/shard_map/dot_general | solution.py:85
  184.1 4.8 pad_maximum_fusion
  188.9 0.0 all-reduce.2.cloned.1.call-update
  188.9 0.0 copy-start.7
  188.9 0.2 reduce-scatter.5.cloned.1.call-start
  189.1 324.6 %all-reduce.2.cloned.1.call-done = f32[512,4608]{1,0:T(8,128)} async-done(((f32[512,4608]{1,0:T(8,128)}), f32[512,4608]{1,0:T(8,128)}) %all-reduce.2.cloned.1.call-update) | async-done | bytes 9437200 | tf_op jit(solution)/shard_map/psum | solution.py:48
  513.7 13.0 %fusion.2 = f32[512,1792]{1,0:T(8,128)} fusion(bf16[2304,1792]{1,0:T(8,128)(2,1)} %param.25, f32[512,4608]{1,0:T(8,128)} %all-reduce.2.cloned.1.call-done), kind=kOutput, calls=%fused_computation.6 | convolution fusion | flops 4234936320 | bytes 21364736 | tf_op jit(solution)/shard_map/dot_general | solution.py:50
  526.7 0.0 reduce-scatter.5.cloned.1.call-update
  526.8 0.6 fusion.27
  527.4 0.6 iota_compare_fusion.1
  528.1 46.6 %reduce-scatter.5.cloned.1.call-done = f32[64,1792]{1,0:T(8,128)} async-done(((f32[512,1792]{1,0:T(8,128)}), f32[64,1792]{1,0:T(8,128)}) %reduce-scatter.5.cloned.1.call-update) | async-done | bytes 458768 | tf_op jit(solution)/shard_map/reduce_scatter | solution.py:88
  574.7 1.8 fusion.24
  (6 shorter events, 0.0 us)
Async XLA Ops:
  6.5 6.9 %copy-start = (bf16[64,4096]{1,0:T(8,128)(2,1)S(1)}, bf16[64,4096]{1,0:T(8,128)(2,1)}, u32[]{:S(2)}) copy-start(bf16[64,4096]{1,0:T(8,128)(2,1)} %param.14) | copy-start | bytes 1572868
  6.5 49.4 %all-gather.3.cloned.1.call-start = ((), (), s32[]{:S(2)}) async-start(), calls=%async_computation.3 | async-start | bytes 4718592 | tf_op jit(solution)/shard_map/all_gather | solution.py:73
  10.2 3.9 copy-start.2
  10.2 3.9 copy-start.3
  16.4 115.9 %reduce-scatter.3.cloned.1.call-start = ((), (), s32[]{:S(2)}) async-start(), calls=%async_computation.4 | async-start | bytes 2293760 | tf_op jit(solution)/shard_map/reduce_scatter | solution.py:78
  65.8 66.6 %copy-start.4 = (bf16[64,1792]{1,0:T(8,128)(2,1)S(1)}, bf16[64,1792]{1,0:T(8,128)(2,1)}, u32[]{:S(2)}) copy-start(bf16[64,1792]{1,0:T(8,128)(2,1)} %param.21) | copy-start | bytes 688132
  65.8 77.8 %copy-start.5 = (f32[1792]{0:T(1024)S(1)}, f32[1792]{0:T(1024)}, u32[]{:S(2)}) copy-start(f32[1792]{0:T(1024)} %param.22) | copy-start | bytes 21508
  93.7 75.7 %all-gather.5.cloned.1.call-start = ((), (), s32[]{:S(2)}) async-start(), calls=%async_computation.5 | async-start | bytes 2064384 | tf_op jit(solution)/shard_map/all_gather | solution.py:83
  144.4 369.2 %all-reduce.2.cloned.1.call-start = ((), (), s32[]{:S(2)}) async-start(), calls=%async_computation.6 | async-start | bytes 18874368 | tf_op jit(solution)/shard_map/psum | solution.py:48
  169.3 7.9 %copy-start.6 = (bf16[512,1792]{1,0:T(8,128)(2,1)S(1)}, bf16[512,1792]{1,0:T(8,128)(2,1)}, u32[]{:S(2)}) copy-start(bf16[512,1792]{1,0:T(8,128)(2,1)} %all-gather.5.cloned.1.call-done) | copy-start | bytes 5505028
  188.9 337.9 %copy-start.7 = (s32[8]{0:T(128)S(1)}, s32[8]{0:T(128)}, u32[]{:S(2)}) copy-start(s32[8]{0:T(128)} %param.26) | copy-start | bytes 100
  188.9 385.7 %reduce-scatter.5.cloned.1.call-start = ((), (), s32[]{:S(2)}) async-start(), calls=%async_computation.7 | async-start | bytes 4128768 | tf_op jit(solution)/shard_map/reduce_scatter | solution.py:88
  513.7 62.8 %copy-start.1 = (bf16[64,4096]{1,0:T(8,128)(2,1)S(1)}, bf16[64,4096]{1,0:T(8,128)(2,1)}, u32[]{:S(2)}) copy-start(bf16[64,4096]{1,0:T(8,128)(2,1)} %param.14) | copy-start | bytes 1572868
Sparse Core Ops, SparseCore 0:
  16.5 39.4 all-gather.2
  93.8 38.5 reduce-scatter.2
  144.6 24.7 all-gather.4
  189.0 324.6 all-reduce.1
  526.9 47.7 reduce-scatter.4
where the time goes:
time: 583 us
  waiting for transfers between devices  474 us (81%)
  matrix products  43.8 us (8%)
  blocking collectives  36.5 us (6%)
  between operations  13.3 us (2%)
  other arithmetic  11 us (2%)
    psum x1, waiting for transfers between devices, feed_forward(): totals = lax.psum(partial_gate, 'hd')  325 us
    reduce_scatter x1, waiting for transfers between devices, on_device(): mlp = lax.psum_scatter(down_rows, 'dp', scatter_dimension=0, tiled=True)  46.6 us
    all_gather x1, waiting for transfers between devices, on_device(): lax.all_gather(attended, 'dp', axis=0, tiled=True)  39.5 us
    reduce_scatter x1, waiting for transfers between devices, on_device(): lax.psum_scatter(by_token, 'hd', scatter_dimension=1, tiled=True)  38.6 us
    all_to_all x1, blocking collectives, on_device(): lax.all_to_all(partial_proj, 'dp', split_axis=0, concat_axis=1, tiled=True)  26.5 us
    all_gather x1, waiting for transfers between devices, on_device(): piece = lax.all_gather(normed, 'dp', axis=0, tiled=True)  24.8 us
    dot_general x1, matrix products, feed_forward(): return jnp.dot(hidden, down_weight, preferred_element_type=jnp.float32)  13 us
  transfers between devices with their start and end apart: 5, of which 5 were waited for; matrix products, arithmetic and copies ran while one was open for 0% of the time, Pallas kernels for 0%

commit v1 on v0

v1 whole, which is shorter than its diff:
```python
import functools

import jax
import jax.numpy as jnp
from jax import lax
from jax.experimental import pallas as pl
from jax.experimental.pallas import tpu as pltpu
from jax.sharding import PartitionSpec as P

NOPE = 128
ROPE = 64
VH = 128
MESH = pl.DeviceIdType.MESH


def attend(query_nope, query_rope, latent, key_rope, key_up, value_up, request_row):
    slots = latent.shape[0]
    heads = key_up.shape[1] // NOPE
    key_nope = jnp.dot(latent, key_up, preferred_element_type=jnp.float32).astype(jnp.bfloat16)
    values = jnp.dot(latent, value_up, preferred_element_type=jnp.float32).astype(jnp.bfloat16)
    query_heads = query_nope.reshape(slots, heads, NOPE)
    rotary_heads = query_rope.reshape(slots, heads, ROPE)
    scores = jnp.einsum(
        "shd,thd->hst",
        query_heads,
        key_nope.reshape(slots, heads, NOPE),
        preferred_element_type=jnp.float32,
    )
    scores = scores + jnp.einsum(
        "shd,td->hst", rotary_heads, key_rope, preferred_element_type=jnp.float32
    )
    scores = scores * (NOPE + ROPE) ** (-0.5)
    position = jnp.arange(slots, dtype=jnp.int32)
    allowed = (request_row[:, None] == request_row[None, :]) & (
        position[None, :] <= position[:, None]
    )
    scores = jnp.where(allowed[None, :, :], scores, jnp.float32(-1e30))
    top = jnp.max(scores, axis=-1, keepdims=True)
    raised = jnp.exp(scores - top)
    weights = (raised / jnp.sum(raised, axis=-1, keepdims=True)).astype(jnp.bfloat16)
    attended = jnp.einsum(
        "hst,thd->shd",
        weights,
        values.reshape(slots, heads, VH),
        preferred_element_type=jnp.float32,
    )
    return attended.astype(jnp.bfloat16).reshape(slots, heads * VH)


def f32_dot(a, b):
    return jnp.dot(a, b, preferred_element_type=jnp.float32)


def layer_kernel(
    n,
    m,
    att,
    res,
    gain,
    pack,
    unpack,
    wo_hbm,
    wg_hbm,
    wu_hbm,
    wd_hbm,
    out,
    wo,
    wg,
    wu,
    wd,
    gathered,
    packed,
    res_all,
    part,
    from_low,
    from_high,
    mixed,
    scaled,
    squares,
    squares_all,
    gu,
    gu_low,
    gu_high,
    hidden,
    y,
    y_pair,
    pair_in,
    y_own,
    chip_in,
    w_sem,
    own_sem,
    ag_ring_send,
    ag_pair_send,
    ag_recv,
    res_send,
    res_recv,
    line_send,
    line_low,
    line_high,
    bc_ring_send,
    bc_pair_send,
    bc_recv,
    sq_send,
    sq_recv,
    gu_send,
    gu_low_recv,
    gu_high_recv,
    hid_send_up,
    hid_send_down,
    hid_recv,
    pair_send,
    pair_recv,
    chip_send,
    chip_recv,
):
    i, j = lax.axis_index("dp"), lax.axis_index("hd")
    chips = n // 2
    chip, core = i // 2, lax.rem(i, 2)
    sibling = i + 1 - 2 * core
    side = 1
    while side * side < chips:
        side *= 2
    nb, rows, width = mixed.shape
    tiles = gu.shape[0]
    tile = gu.shape[2] // 2
    mine = rows // m
    quarters = from_low.shape[0]
    step_rows = rows // quarters
    half_f = packed.shape[2]
    slots = att.shape[1]

    def place(c):
        a, b = c // side, lax.rem(c, side)
        return a * side + b + lax.rem(a, 2) * (side - 1 - 2 * b)

    def chip_at(k):
        k = lax.rem(k + 2 * chips, chips)
        a, b = k // side, lax.rem(k, side)
        return a * side + b + lax.rem(a, 2) * (side - 1 - 2 * b)

    here = place(chip)
    after, before = 2 * chip_at(here + 1) + core, 2 * chip_at(here - 1) + core

    def send(src, dst, s_sem, r_sem, dp, hd):
        copy = pltpu.make_async_remote_copy(
            src_ref=src,
            dst_ref=dst,
            send_sem=s_sem,
            recv_sem=r_sem,
            device_id={"dp": dp, "hd": hd},
            device_id_type=MESH,
        )
        copy.start()

    def landed(ref, r_sem):
        pltpu.make_async_copy(ref, ref, r_sem).wait()

    loads = []
    for q, (a, b) in enumerate(((wo_hbm, wo), (wg_hbm, wg), (wu_hbm, wu), (wd_hbm, wd))):
        load = pltpu.make_async_copy(a, b, w_sem.at[q])
        load.start()
        loads.append(load)

    barrier = pltpu.get_barrier_semaphore()
    for d in range(1, n):
        pl.semaphore_signal(
            barrier, inc=1, device_id={"dp": lax.rem(i + d, n), "hd": j}, device_id_type=MESH
        )
    for d in range(1, m):
        pl.semaphore_signal(
            barrier, inc=1, device_id={"dp": i, "hd": lax.rem(j + d, m)}, device_id_type=MESH
        )
    pl.semaphore_wait(barrier, n + m - 2)

    for h in range(2):
        send(
            att.at[h],
            gathered.at[h, i],
            ag_ring_send.at[h, 0],
            ag_recv.at[h, i],
            (after, before)[h],
            j,
        )
    for h in range(2):
        send(att.at[h], gathered.at[h, i], ag_pair_send.at[h, 0], ag_recv.at[h, i], sibling, j)
        pltpu.make_async_copy(att.at[h], gathered.at[h, i], own_sem.at[h]).start()
    for b in range(nb):
        target = j * nb + b

        @pl.when(target != i)
        def _():
            send(res.at[b], res_all.at[i], res_send.at[b], res_recv.at[i], target, j)

        @pl.when(target == i)
        def _():
            pltpu.make_async_copy(res.at[b], res_all.at[i], res_send.at[b]).start()

    for step in range(1, chips):
        for h in range(2):
            block = 2 * chip_at(here - step if h == 0 else here + step) + core
            landed(gathered.at[h, block], ag_recv.at[h, block])
            if step < chips - 1:
                send(
                    gathered.at[h, block],
                    gathered.at[h, block],
                    ag_ring_send.at[h, step],
                    ag_recv.at[h, block],
                    (after, before)[h],
                    j,
                )
            send(
                gathered.at[h, block],
                gathered.at[h, block],
                ag_pair_send.at[h, step],
                ag_recv.at[h, block],
                sibling,
                j,
            )
    for h in range(2):
        pltpu.make_async_copy(att.at[h], gathered.at[h, i], own_sem.at[h]).wait()
        for c in range(chips):
            block = 2 * c + 1 - core
            landed(gathered.at[h, block], ag_recv.at[h, block])
    for h in range(2):
        packed[h] = f32_dot(pack[...], gathered[h].reshape(n * slots, half_f)).astype(jnp.bfloat16)
    loads[0].wait()
    part[...] = (
        f32_dot(packed[0], wo[:half_f, :]) + f32_dot(packed[1], wo[half_f:, :])
    ).astype(jnp.bfloat16)

    target = i // nb
    slot = lax.rem(i, nb)

    def bc_forward(b, q, source_chip):
        up = q < quarters // 2
        far = lax.rem((here - place(source_chip) if up else place(source_chip) - here) + chips, chips)

        @pl.when(far < chips - 1)
        def _():
            sl = mixed.at[b, pl.ds(q * step_rows, step_rows)]
            send(sl, sl, bc_ring_send.at[b // 2, q], bc_recv.at[b, q], after if up else before, j)

    @pl.when(j == target)
    def _():
        for k in range(n):
            @pl.when(k != i)
            def _():
                landed(res_all.at[k], res_recv.at[k])

        pltpu.make_async_copy(res.at[slot], res_all.at[i], res_send.at[slot]).wait()
        base = f32_dot(pack[...], res_all[...].reshape(n * slots, width))
        mixed[slot] = base.astype(jnp.bfloat16)

    for q in [x for p in range(quarters // 2) for x in (p, p + quarters // 2)]:
        sl = pl.ds(q * step_rows, step_rows)

        @pl.when(jnp.logical_and(j > 0, j <= target))
        def _():
            landed(from_low.at[q], line_low.at[q])

        @pl.when(jnp.logical_and(j < m - 1, j >= target))
        def _():
            landed(from_high.at[q], line_high.at[q])

        @pl.when(jnp.logical_and(j > 0, j < target))
        def _():
            part[sl] = (part[sl].astype(jnp.float32) + from_low[q].astype(jnp.float32)).astype(
                jnp.bfloat16
            )

        @pl.when(jnp.logical_and(j < m - 1, j > target))
        def _():
            part[sl] = (part[sl].astype(jnp.float32) + from_high[q].astype(jnp.float32)).astype(
                jnp.bfloat16
            )

        @pl.when(j < target)
        def _():
            send(part.at[sl], from_low.at[q], line_send.at[q], line_low.at[q], i, j + 1)

        @pl.when(j > target)
        def _():
            send(part.at[sl], from_high.at[q], line_send.at[q], line_high.at[q], i, j - 1)

        @pl.when(j == target)
        def _():
            total = mixed[slot, sl].astype(jnp.float32) + part[sl].astype(jnp.float32)
            mixed[slot, sl] = total.astype(jnp.bfloat16)

            @pl.when(j > 0)
            def _():
                mixed[slot, sl] = (
                    mixed[slot, sl].astype(jnp.float32) + from_low[q].astype(jnp.float32)
                ).astype(jnp.bfloat16)

            @pl.when(j < m - 1)
            def _():
                mixed[slot, sl] = (
                    mixed[slot, sl].astype(jnp.float32) + from_high[q].astype(jnp.float32)
                ).astype(jnp.bfloat16)

            bc_forward(slot, q, chip)
            view = mixed.at[slot, sl]
            send(view, view, bc_pair_send.at[slot // 2, q], bc_recv.at[slot, q], sibling, j)

    for q in [x for p in range(quarters // 2) for x in (p, p + quarters // 2)]:
        sl = pl.ds(q * step_rows, step_rows)
        for bb in range(nb // 2):
            b = 2 * bb + core
            source = (j * nb + b) // 2

            @pl.when(source != chip)
            def _():
                view = mixed.at[b, sl]
                landed(view, bc_recv.at[b, q])
                bc_forward(b, q, source)
                send(view, view, bc_pair_send.at[bb, q], bc_recv.at[b, q], sibling, j)

    for q in range(quarters):
        sl = pl.ds(q * step_rows, step_rows)
        for bb in range(nb // 2):
            b = 2 * bb + 1 - core
            landed(mixed.at[b, sl], bc_recv.at[b, q])

    total = jnp.zeros((rows, 1), jnp.float32)
    for b in range(nb):
        wide = mixed[b].astype(jnp.float32)
        scaled[b] = (wide * gain[b]).astype(jnp.bfloat16)
        total = total + jnp.sum(wide * wide, axis=1, keepdims=True)
    squares[...] = jnp.broadcast_to(total, squares.shape)
    for d in range(1, m):
        p = lax.rem(j + d, m)
        send(
            squares.at[pl.ds(p * mine, mine)],
            squares_all.at[j],
            sq_send.at[d],
            sq_recv.at[j],
            i,
            p,
        )
    loads[1].wait()
    loads[2].wait()
    for t in range(tiles):
        cols = slice(t * tile, (t + 1) * tile)
        gate = f32_dot(scaled[0], wg[:width, cols])
        up = f32_dot(scaled[0], wu[:width, cols])
        for b in range(1, nb):
            gate = gate + f32_dot(scaled[b], wg[b * width : (b + 1) * width, cols])
            up = up + f32_dot(scaled[b], wu[b * width : (b + 1) * width, cols])
        gu[t, :, :tile] = gate.astype(jnp.bfloat16)
        gu[t, :, tile:] = up.astype(jnp.bfloat16)
        if t == 0:
            pass

        for s in range(m - 1):
            p_up, p_down = m - 1 - s, s
            rows_up, rows_down = pl.ds(p_up * mine, mine), pl.ds(p_down * mine, mine)

            @pl.when(j < p_up)
            def _():
                @pl.when(j > 0)
                def _():
                    landed(gu_low.at[t, p_up], gu_low_recv.at[t, p_up])
                    gu[t, rows_up] = (
                        gu[t, rows_up].astype(jnp.float32) + gu_low[t, p_up].astype(jnp.float32)
                    ).astype(jnp.bfloat16)

                send(
                    gu.at[t, rows_up],
                    gu_low.at[t, p_up],
                    gu_send.at[t, p_up],
                    gu_low_recv.at[t, p_up],
                    i,
                    j + 1,
                )

            @pl.when(j > p_down)
            def _():
                @pl.when(j < m - 1)
                def _():
                    landed(gu_high.at[t, p_down], gu_high_recv.at[t, p_down])
                    gu[t, rows_down] = (
                        gu[t, rows_down].astype(jnp.float32)
                        + gu_high[t, p_down].astype(jnp.float32)
                    ).astype(jnp.bfloat16)

                send(
                    gu.at[t, rows_down],
                    gu_high.at[t, p_down],
                    gu_send.at[t, p_down],
                    gu_high_recv.at[t, p_down],
                    i,
                    j - 1,
                )

    own = pl.ds(pl.multiple_of(j * mine, mine), mine)
    square = squares[own, :1]
    for d in range(1, m):
        p = lax.rem(j + d, m)
        landed(squares_all.at[p], sq_recv.at[p])
        square = square + squares_all[p, :, :1]
    scale = lax.rsqrt(square / (m * nb * width) + 1e-06)
    for t in range(tiles):
        @pl.when(j > 0)
        def _():
            landed(gu_low.at[t, j], gu_low_recv.at[t, j])
            gu[t, own] = (
                gu[t, own].astype(jnp.float32) + gu_low[t, j].astype(jnp.float32)
            ).astype(jnp.bfloat16)

        @pl.when(j < m - 1)
        def _():
            landed(gu_high.at[t, j], gu_high_recv.at[t, j])
            gu[t, own] = (
                gu[t, own].astype(jnp.float32) + gu_high[t, j].astype(jnp.float32)
            ).astype(jnp.bfloat16)

        gate = gu[t, own, :tile].astype(jnp.float32) * scale
        up = gu[t, own, tile:].astype(jnp.float32) * scale
        hidden[t, j] = (gate / (1.0 + jnp.exp(-gate)) * up).astype(jnp.bfloat16)

        view = hidden.at[t, j]

        @pl.when(j < m - 1)
        def _():
            send(view, view, hid_send_up.at[t, j], hid_recv.at[t, j], i, j + 1)

        @pl.when(j > 0)
        def _():
            send(view, view, hid_send_down.at[t, j], hid_recv.at[t, j], i, j - 1)

    for s in range(1, m):
        for t in range(tiles):
            @pl.when(j >= s)
            def _():
                view = hidden.at[t, j - s]
                landed(view, hid_recv.at[t, j - s])

                @pl.when(j < m - 1)
                def _():
                    send(view, view, hid_send_up.at[t, j - s], hid_recv.at[t, j - s], i, j + 1)

            @pl.when(j + s <= m - 1)
            def _():
                view = hidden.at[t, j + s]
                landed(view, hid_recv.at[t, j + s])

                @pl.when(j > 0)
                def _():
                    send(view, view, hid_send_down.at[t, j + s], hid_recv.at[t, j + s], i, j - 1)

    loads[3].wait()
    total = f32_dot(hidden[0].reshape(rows, tile), wd[:tile, :])
    for t in range(1, tiles):
        total = total + f32_dot(hidden[t].reshape(rows, tile), wd[t * tile : (t + 1) * tile, :])
    y[...] = total.astype(jnp.bfloat16)

    for d in range(chips):
        c = lax.rem(chip + d + 1, chips)
        y_pair[c] = f32_dot(unpack[2 * c + 1 - core], y[...]).astype(jnp.bfloat16)
        send(y_pair.at[c], pair_in.at[c], pair_send.at[c], pair_recv.at[c], sibling, j)
    for d in range(chips):
        c = lax.rem(chip + d + 1, chips)
        mine_rows = f32_dot(unpack[2 * c + core], y[...])
        landed(pair_in.at[c], pair_recv.at[c])
        y_own[c] = (mine_rows + pair_in[c].astype(jnp.float32)).astype(jnp.bfloat16)
        if d < chips - 1:
            send(
                y_own.at[c], chip_in.at[chip], chip_send.at[c], chip_recv.at[chip], 2 * c + core, j
            )
    kept = jnp.concatenate([f32_dot(unpack[i], mixed[b]) for b in range(nb)], axis=1)
    kept = kept + y_own[chip].astype(jnp.float32)
    for d in range(1, chips):
        c = lax.rem(chip + d, chips)
        landed(chip_in.at[c], chip_recv.at[c])
        kept = kept + chip_in[c].astype(jnp.float32)
    out[...] = kept.astype(jnp.bfloat16)

    def sent(ref, sem):
        pltpu.make_async_copy(ref, ref, sem).wait()

    for h in range(2):
        for step in range(chips):
            if step < chips - 1:
                sent(att.at[h], ag_ring_send.at[h, step])
            sent(att.at[h], ag_pair_send.at[h, step])
    for b in range(nb):
        @pl.when(j * nb + b != i)
        def _():
            sent(res.at[b], res_send.at[b])
    for q in range(quarters):
        @pl.when(j != target)
        def _():
            sent(from_low.at[q], line_send.at[q])

        for bb in range(nb // 2):
            source = (j * nb + 2 * bb + core) // 2
            up = q < quarters // 2
            far = lax.rem((here - place(source) if up else place(source) - here) + chips, chips)

            @pl.when(far < chips - 1)
            def _():
                sent(from_low.at[q], bc_ring_send.at[bb, q])

            sent(from_low.at[q], bc_pair_send.at[bb, q])
    for d in range(1, m):
        sent(squares_all.at[0], sq_send.at[d])
    for t in range(tiles):
        for p in range(m):
            @pl.when(p != j)
            def _():
                sent(gu_low.at[t, p], gu_send.at[t, p])

            @pl.when(jnp.logical_and(p <= j, j < m - 1))
            def _():
                sent(hidden.at[t, p], hid_send_up.at[t, p])

            @pl.when(jnp.logical_and(p >= j, j > 0))
            def _():
                sent(hidden.at[t, p], hid_send_down.at[t, p])
    for c in range(chips):
        sent(y_pair.at[c], pair_send.at[c])

        @pl.when(c != chip)
        def _():
            sent(y_own.at[c], chip_send.at[c])


def rest(att, res, gain, pack, unpack, wo, wg, wu, wd):
    n, m = lax.axis_size("dp"), lax.axis_size("hd")
    _, slots, half_f = att.shape
    nb, _, width = res.shape
    rows = pack.shape[0]
    features = wd.shape[1]
    units = wd.shape[0]
    tiles = 3 if units % 384 == 0 else 1
    tile = units // tiles
    quarters = 4
    chips = n // 2
    mine = rows // m
    bf, f32 = jnp.bfloat16, jnp.float32
    vmem = pl.BlockSpec(memory_space=pltpu.VMEM)
    hbm = pl.BlockSpec(memory_space=pl.ANY)
    dma = pltpu.SemaphoreType.DMA
    step_rows = rows // quarters
    scratch = [
        pltpu.VMEM(wo.shape, bf),
        pltpu.VMEM(wg.shape, bf),
        pltpu.VMEM(wu.shape, bf),
        pltpu.VMEM(wd.shape, bf),
        pltpu.VMEM((2, n, slots, half_f), bf),
        pltpu.VMEM((2, rows, half_f), bf),
        pltpu.VMEM((n, slots, width), bf),
        pltpu.VMEM((rows, width), bf),
        pltpu.VMEM((quarters, step_rows, width), bf),
        pltpu.VMEM((quarters, step_rows, width), bf),
        pltpu.VMEM((nb, rows, width), bf),
        pltpu.VMEM((nb, rows, width), bf),
        pltpu.VMEM((rows, 128), f32),
        pltpu.VMEM((m, mine, 128), f32),
        pltpu.VMEM((tiles, rows, 2 * tile), bf),
        pltpu.VMEM((tiles, m, mine, 2 * tile), bf),
        pltpu.VMEM((tiles, m, mine, 2 * tile), bf),
        pltpu.VMEM((tiles, m, mine, tile), bf),
        pltpu.VMEM((rows, features), bf),
        pltpu.VMEM((chips, slots, features), bf),
        pltpu.VMEM((chips, slots, features), bf),
        pltpu.VMEM((chips, slots, features), bf),
        pltpu.VMEM((chips, slots, features), bf),
        dma((4,)),
        dma((2,)),
        dma((2, chips)),
        dma((2, chips)),
        dma((2, n)),
        dma((nb,)),
        dma((n,)),
        dma((quarters,)),
        dma((quarters,)),
        dma((quarters,)),
        dma((nb // 2, quarters)),
        dma((nb // 2, quarters)),
        dma((nb, quarters)),
        dma((m,)),
        dma((m,)),
        dma((tiles, m)),
        dma((tiles, m)),
        dma((tiles, m)),
        dma((tiles, m)),
        dma((tiles, m)),
        dma((tiles, m)),
        dma((chips,)),
        dma((chips,)),
        dma((chips,)),
        dma((chips,)),
    ]
    return pl.pallas_call(
        functools.partial(layer_kernel, n, m),
        out_shape=jax.ShapeDtypeStruct((slots, features), bf),
        in_specs=[vmem] * 5 + [hbm] * 4,
        out_specs=vmem,
        scratch_shapes=scratch,
        compiler_params=pltpu.CompilerParams(
            collective_id=0, has_side_effects=True, vmem_limit_bytes=60 * 1024 * 1024
        ),
        cost_estimate=pl.CostEstimate(
            flops=2 * rows * (wo.size + wg.size + wu.size + wd.size),
            bytes_accessed=2 * (wo.size + wg.size + wu.size + wd.size),
            transcendentals=0,
        ),
    )(att, res, gain, pack, unpack, wo, wg, wu, wd)


def on_device(
    query_nope,
    query_rope,
    latent,
    key_rope,
    key_up,
    value_up,
    output_weight,
    residual,
    norm_gain,
    gate_weight,
    up_weight,
    down_weight,
    rank_tokens,
    request_ids,
):
    slots = latent.shape[0]
    n, m = lax.axis_size("dp"), lax.axis_size("hd")
    nb = n // m
    attended = attend(query_nope, query_rope, latent, key_rope, key_up, value_up, request_ids[0])
    att = attended.reshape(slots, 2, -1).transpose(1, 0, 2)
    res = residual.reshape(slots, nb, -1).transpose(1, 0, 2)
    gain = norm_gain.reshape(nb, 1, -1)
    rows = n * slots // 2
    first = jnp.cumsum(rank_tokens) - rank_tokens
    slot = jnp.arange(slots, dtype=jnp.int32)
    packed_row = jnp.where(
        slot[None, :] < rank_tokens[:, None], first[:, None] + slot[None, :], -1
    )
    row = jnp.arange(rows, dtype=jnp.int32)
    pack = (row[:, None] == packed_row.reshape(1, -1)).astype(jnp.bfloat16)
    unpack = (packed_row[:, :, None] == row[None, None, :]).astype(jnp.bfloat16)
    return rest(
        att, res, gain, pack, unpack, output_weight, gate_weight, up_weight, down_weight
    )


def solution(mesh):
    in_specs = (
        P("dp", "hd"),
        P("dp", "hd"),
        P("dp", None),
        P("dp", None),
        P(None, "hd"),
        P(None, "hd"),
        P("hd", "dp"),
        P("dp", "hd"),
        P("hd"),
        P("hd", "dp"),
        P("hd", "dp"),
        P("dp", "hd"),
        P(),
        P("dp", None),
    )
    out_specs = P("dp", "hd")
    return jax.shard_map(
        on_device, mesh=mesh, in_specs=in_specs, out_specs=out_specs, check_vma=False
    )
```

time: 583 us -> 188 us (0.32)
  waiting for transfers between devices: 474 us -> 0 us
  Pallas kernels: 0 us -> 173 us
  matrix products: 43.8 us -> 6.27 us
  blocking collectives: 36.5 us -> 0 us
  between operations: 13.3 us -> 0.13 us
  other arithmetic: 11 us -> 2.21 us
    psum x1 -> x0, waiting for transfers between devices: 325 us -> none  [feed_forward(): totals = lax.psum(partial_gate, 'hd')]
    pallas_call x0 -> x1, Pallas kernels: none -> 173 us  [rest(): pl.pallas_call(functools.partial(layer_kernel, n, m), out_shape=jax.Shape...]
    reduce_scatter x2 -> x0, waiting for transfers between devices: 85.2 us -> none  [the longest x1 46.6 us: on_device(): mlp = lax.psum_scatter(down_rows, 'dp', scatter_dimension=0, tiled=True)]
    all_gather x2 -> x0, waiting for transfers between devices: 64.4 us -> none  [the longest x1 39.5 us: on_device(): lax.all_gather(attended, 'dp', axis=0, tiled=True)]
    dot_general x4 -> x0, matrix products: 37.5 us -> none  [the longest x1 13 us: feed_forward(): return jnp.dot(hidden, down_weight, preferred_element_type=jnp.float32)]
    all_to_all x1 -> x0, blocking collectives: 26.5 us -> none  [on_device(): lax.all_to_all(partial_proj, 'dp', split_axis=0, concat_axis=1, tiled=True)]
    psum x1 -> x0, blocking collectives: 10 us -> none  [on_device(): square_sum = lax.psum(jnp.sum(widened * widened, axis=1), 'hd')]
  transfers between devices with their start and end apart: 5 -> 0, of which waited for: 5 -> 0; matrix products, arithmetic and copies ran while one was open for 0% -> 0% of each run, Pallas kernels for 0% -> 0%
where the time goes in v1:
time: 188 us
  Pallas kernels  173 us (92%)
  matrix products  6.27 us (3%)
  local copies, waits for them, and re-layouts  6.02 us (3%)
  other arithmetic  2.21 us (1%)
    pallas_call x1, Pallas kernels, rest(): pl.pallas_call(functools.partial(layer_kernel, n, m), out_shape=jax.Shape...  173 us

profile of v1, /device:TPU:0, one launch (start us, length us, event | category | flops | bytes accessed | tf_op | source)
XLA Modules:
  0.0 187.7 jit_solution(6676380439019142295)
XLA Ops:
  0.0 0.0 copy-start
  0.0 0.0 copy-start.5
  0.0 1.5 reshape.165
  1.5 1.4 convolution_bitcast_fusion
  2.9 0.0 copy-start.1
  2.9 0.0 copy-start.2
  2.9 3.2 %fusion.7 = bf16[8,32,8,128]{3,2,1,0:T(8,128)(2,1)S(1)} fusion(bf16[64,512]{1,0:T(8,128)(2,1)} %param.16, bf16[512,4096]{1,0:T(8,128)(2,1)} %param.18), kind=kOutput, calls=%fused_computation.12 | convolution fusion | flops 268697600 | bytes 4784128 | tf_op jit(solution)/shard_map/dot_general | solution.py:19
  6.1 0.0 copy-done.5
  6.2 0.1 fusion.19
  6.2 0.0 copy-done
  6.2 0.4 fusion.5
  6.7 0.3 fusion.22
  6.9 0.0 copy-done.1
  6.9 0.0 copy-done.2
  6.9 0.8 fusion.6
  7.8 0.0 copy-start.6
  7.8 0.0 copy-start.3
  7.8 0.0 copy-start.4
  7.8 0.5 fusion.8
  8.3 0.3 copy.25
  8.6 0.1 reshape_reshape.3
  8.8 0.9 copy.49
  9.7 0.0 copy-done.6
  9.7 0.2 reduce-window.9
  9.9 0.1 add_select_fusion
  10.0 0.1 select_n.21
  10.1 0.8 fusion.17.pack
  10.8 0.8 fusion.18.unpack
  11.7 0.0 copy-done.3
  11.7 0.7 copy.50
  12.4 0.0 copy-done.4
  12.4 0.6 reshape.167.gain
  13.0 173.0 %shard_map.136 = bf16[64,1792]{1,0:T(8,128)(2,1)} custom-call(bf16[2,64,2048]{2,1,0:T(8,128)(2,1)} %bitcast.52, bf16[2,64,896]{2,1,0:T(8,128)(2,1)} %bitcast.53, f32[2,1,896]{2,1,0:T(1,128)} %reshape.167.gain, bf16[256,512]{1,0:T(8,128)(2,1)} %fusion.17.pack, bf16[8,64,256]{2,1,0:T(8,128)(2,1)} %fusion.18.unpack, bf16[4096,896]{1,0:T(8,128)(2,1)} %wo_hbm.1, ...), custom_call_target="tpu_custom_call" | custom-call | flops 8220835840 | bytes 32112640 | tf_op jit(solution)/shard_map/pallas_call | solution.py:596
  186.0 1.6 copy.52
  (1 shorter events, 0.0 us)
Async XLA Ops:
  0.0 6.2 %copy-start = (bf16[64,4096]{1,0:T(8,128)(2,1)S(1)}, bf16[64,4096]{1,0:T(8,128)(2,1)}, u32[]{:S(2)}) copy-start(bf16[64,4096]{1,0:T(8,128)(2,1)} %param.14) | copy-start | bytes 1572868
  0.0 6.1 %copy-start.5 = (s32[1,64]{1,0:T(1,128)S(1)}, s32[1,64]{1,0:T(1,128)}, u32[]{:S(2)}) copy-start(s32[1,64]{1,0:T(1,128)} %param.27) | copy-start | bytes 772
  2.9 4.0 %copy-start.1 = (bf16[512,4096]{1,0:T(8,128)(2,1)S(1)}, bf16[512,4096]{1,0:T(8,128)(2,1)}, u32[]{:S(2)}) copy-start(bf16[512,4096]{1,0:T(8,128)(2,1)} %param.19) | copy-start | bytes 12582916
  2.9 4.0 %copy-start.2 = (bf16[64,512]{1,0:T(8,128)(2,1)S(1)}, bf16[64,512]{1,0:T(8,128)(2,1)}, u32[]{:S(2)}) copy-start(bf16[64,512]{1,0:T(8,128)(2,1)} %param.16) | copy-start | bytes 196612
  7.8 1.9 %copy-start.6 = (s32[8]{0:T(128)S(1)}, s32[8]{0:T(128)}, u32[]{:S(2)}) copy-start(s32[8]{0:T(128)} %param.26) | copy-start | bytes 100
  7.8 3.9 %copy-start.3 = (bf16[64,1792]{1,0:T(8,128)(2,1)S(1)}, bf16[64,1792]{1,0:T(8,128)(2,1)}, u32[]{:S(2)}) copy-start(bf16[64,1792]{1,0:T(8,128)(2,1)} %param.21) | copy-start | bytes 688132
  7.8 4.6 %copy-start.4 = (f32[1792]{0:T(1024)S(1)}, f32[1792]{0:T(1024)}, u32[]{:S(2)}) copy-start(f32[1792]{0:T(1024)} %param.22) | copy-start | bytes 21508

commit v2 on v1

--- a/solution.py
+++ b/solution.py
@@ -69,7 +69,7 @@
     wu,
     wd,
     gathered,
-    packed,
+    acc,
     res_all,
     part,
     from_low,
@@ -79,8 +79,7 @@
     squares,
     squares_all,
     gu,
-    gu_low,
-    gu_high,
+    gu_in,
     hidden,
     y,
     y_pair,
@@ -103,8 +102,7 @@
     sq_send,
     sq_recv,
     gu_send,
-    gu_low_recv,
-    gu_high_recv,
+    gu_recv,
     hid_send_up,
     hid_send_down,
     hid_recv,
@@ -122,12 +120,18 @@
         side *= 2
     nb, rows, width = mixed.shape
     tiles = gu.shape[0]
-    tile = gu.shape[2] // 2
+    tile = gu.shape[3] // 2
     mine = rows // m
     quarters = from_low.shape[0]
     step_rows = rows // quarters
-    half_f = packed.shape[2]
-    slots = att.shape[1]
+    half_f = gathered.shape[3]
+    slots = att.shape[0]
+
+    def att_half(h):
+        return att.at[:, pl.ds(h * half_f, half_f)]
+
+    def res_block(b):
+        return res.at[:, pl.ds(b * width, width)] if len(res.shape) == 2 else res.at[b]
 
     def place(c):
         a, b = c // side, lax.rem(c, side)
@@ -158,8 +162,11 @@
     loads = []
     for q, (a, b) in enumerate(((wo_hbm, wo), (wg_hbm, wg), (wu_hbm, wu), (wd_hbm, wd))):
         load = pltpu.make_async_copy(a, b, w_sem.at[q])
-        load.start()
+        if q == 0:
+            load.start()
         loads.append(load)
+    from_low[...] = jnp.zeros_like(from_low)
+    from_high[...] = jnp.zeros_like(from_high)
 
     barrier = pltpu.get_barrier_semaphore()
     for d in range(1, n):
@@ -174,7 +181,7 @@
 
     for h in range(2):
         send(
-            att.at[h],
+            att_half(h),
             gathered.at[h, i],
             ag_ring_send.at[h, 0],
             ag_recv.at[h, i],
@@ -182,51 +189,52 @@
             j,
         )
     for h in range(2):
-        send(att.at[h], gathered.at[h, i], ag_pair_send.at[h, 0], ag_recv.at[h, i], sibling, j)
-        pltpu.make_async_copy(att.at[h], gathered.at[h, i], own_sem.at[h]).start()
-    for b in range(nb):
-        target = j * nb + b
-
-        @pl.when(target != i)
-        def _():
-            send(res.at[b], res_all.at[i], res_send.at[b], res_recv.at[i], target, j)
-
-        @pl.when(target == i)
-        def _():
-            pltpu.make_async_copy(res.at[b], res_all.at[i], res_send.at[b]).start()
-
-    for step in range(1, chips):
+        send(att_half(h), gathered.at[h, i], ag_pair_send.at[h, 0], ag_recv.at[h, i], sibling, j)
+        pltpu.make_async_copy(att_half(h), gathered.at[h, i], own_sem.at[h]).start()
+    loads[0].wait()
+    for load in loads[1:]:
+        load.start()
+    for step in range(chips):
+        sources = [chip_at(here - step), chip_at(here + step)]
         for h in range(2):
-            block = 2 * chip_at(here - step if h == 0 else here + step) + core
+            block = 2 * sources[h] + core
+            if step == 0:
+                pltpu.make_async_copy(att_half(h), gathered.at[h, i], own_sem.at[h]).wait()
+                continue
             landed(gathered.at[h, block], ag_recv.at[h, block])
+            view = gathered.at[h, block]
             if step < chips - 1:
                 send(
-                    gathered.at[h, block],
-                    gathered.at[h, block],
+                    view,
+                    view,
                     ag_ring_send.at[h, step],
                     ag_recv.at[h, block],
                     (after, before)[h],
                     j,
                 )
-            send(
-                gathered.at[h, block],
-                gathered.at[h, block],
-                ag_pair_send.at[h, step],
-                ag_recv.at[h, block],
-                sibling,
-                j,
-            )
-    for h in range(2):
-        pltpu.make_async_copy(att.at[h], gathered.at[h, i], own_sem.at[h]).wait()
-        for c in range(chips):
-            block = 2 * c + 1 - core
+            send(view, view, ag_pair_send.at[h, step], ag_recv.at[h, block], sibling, j)
+        if step == chips - 1:
+            for b in range(nb):
+                goal = j * nb + b
+
+                @pl.when(goal != i)
+                def _():
+                    send(res_block(b), res_all.at[i], res_send.at[b], res_recv.at[i], goal, j)
+
+                @pl.when(goal == i)
+                def _():
+                    pltpu.make_async_copy(res_block(b), res_all.at[i], res_send.at[b]).start()
+
+        for h in range(2):
+            block = 2 * sources[h] + 1 - core
             landed(gathered.at[h, block], ag_recv.at[h, block])
-    for h in range(2):
-        packed[h] = f32_dot(pack[...], gathered[h].reshape(n * slots, half_f)).astype(jnp.bfloat16)
-    loads[0].wait()
-    part[...] = (
-        f32_dot(packed[0], wo[:half_f, :]) + f32_dot(packed[1], wo[half_f:, :])
-    ).astype(jnp.bfloat16)
+            both = gathered[h, pl.ds(2 * sources[h], 2)].reshape(2 * slots, half_f)
+            sl = pl.ds(pl.multiple_of(2 * sources[h] * slots, 2 * slots), 2 * slots)
+            term = f32_dot(both, wo[h * half_f : (h + 1) * half_f, :])
+            first = step == 0 and h == 0 or step > 0 and 2 * step < chips
+            first = first or (2 * step == chips and h == 0)
+            acc[sl] = term if first else acc[sl] + term
+    part[...] = f32_dot(pack[...], acc[...].astype(jnp.bfloat16)).astype(jnp.bfloat16)
 
     target = i // nb
     slot = lax.rem(i, nb)
@@ -247,7 +255,7 @@
             def _():
                 landed(res_all.at[k], res_recv.at[k])
 
-        pltpu.make_async_copy(res.at[slot], res_all.at[i], res_send.at[slot]).wait()
+        pltpu.make_async_copy(res_all.at[i], res_all.at[i], res_send.at[slot]).wait()
         base = f32_dot(pack[...], res_all[...].reshape(n * slots, width))
         mixed[slot] = base.astype(jnp.bfloat16)
 
@@ -285,20 +293,8 @@
         @pl.when(j == target)
         def _():
             total = mixed[slot, sl].astype(jnp.float32) + part[sl].astype(jnp.float32)
+            total = total + (from_low[q].astype(jnp.float32) + from_high[q].astype(jnp.float32))
             mixed[slot, sl] = total.astype(jnp.bfloat16)
-
-            @pl.when(j > 0)
-            def _():
-                mixed[slot, sl] = (
-                    mixed[slot, sl].astype(jnp.float32) + from_low[q].astype(jnp.float32)
-                ).astype(jnp.bfloat16)
-
-            @pl.when(j < m - 1)
-            def _():
-                mixed[slot, sl] = (
-                    mixed[slot, sl].astype(jnp.float32) + from_high[q].astype(jnp.float32)
-                ).astype(jnp.bfloat16)
-
             bc_forward(slot, q, chip)
             view = mixed.at[slot, sl]
             send(view, view, bc_pair_send.at[slot // 2, q], bc_recv.at[slot, q], sibling, j)
@@ -325,7 +321,7 @@
     total = jnp.zeros((rows, 1), jnp.float32)
     for b in range(nb):
         wide = mixed[b].astype(jnp.float32)
-        scaled[b] = (wide * gain[b]).astype(jnp.bfloat16)
+        scaled[b] = (wide * gain[:, b * width : (b + 1) * width]).astype(jnp.bfloat16)
         total = total + jnp.sum(wide * wide, axis=1, keepdims=True)
     squares[...] = jnp.broadcast_to(total, squares.shape)
     for d in range(1, m):
@@ -341,84 +337,73 @@
     loads[1].wait()
     loads[2].wait()
     for t in range(tiles):
+        @pl.when(j == 0)
+        def _():
+            gu_in[0, t, 0] = jnp.zeros_like(gu_in[0, t, 0])
+
+        @pl.when(j == m - 1)
+        def _():
+            gu_in[1, t, m - 1] = jnp.zeros_like(gu_in[1, t, m - 1])
+
+    def gate_up(t):
         cols = slice(t * tile, (t + 1) * tile)
         gate = f32_dot(scaled[0], wg[:width, cols])
         up = f32_dot(scaled[0], wu[:width, cols])
         for b in range(1, nb):
             gate = gate + f32_dot(scaled[b], wg[b * width : (b + 1) * width, cols])
             up = up + f32_dot(scaled[b], wu[b * width : (b + 1) * width, cols])
-        gu[t, :, :tile] = gate.astype(jnp.bfloat16)
-        gu[t, :, tile:] = up.astype(jnp.bfloat16)
-        if t == 0:
-            pass
-
+        gu[t, :, :, :tile] = gate.astype(jnp.bfloat16).reshape(m, mine, tile)
+        gu[t, :, :, tile:] = up.astype(jnp.bfloat16).reshape(m, mine, tile)
+
+    def pass_sums(t):
         for s in range(m - 1):
-            p_up, p_down = m - 1 - s, s
-            rows_up, rows_down = pl.ds(p_up * mine, mine), pl.ds(p_down * mine, mine)
-
-            @pl.when(j < p_up)
-            def _():
-                @pl.when(j > 0)
+            for turn in range(2):
+                nearer = (2 * j) // m
+                way = nearer if turn == 0 else 1 - nearer
+                p = (1 - way) * (m - 1 - s) + way * s
+                ahead = 1 - 2 * way
+                come = (1 - way) * j + way * (m - 1 - j)
+
+                @pl.when((p - j) * ahead > 0)
                 def _():
-                    landed(gu_low.at[t, p_up], gu_low_recv.at[t, p_up])
-                    gu[t, rows_up] = (
-                        gu[t, rows_up].astype(jnp.float32) + gu_low[t, p_up].astype(jnp.float32)
-                    ).astype(jnp.bfloat16)
-
-                send(
-                    gu.at[t, rows_up],
-                    gu_low.at[t, p_up],
-                    gu_send.at[t, p_up],
-                    gu_low_recv.at[t, p_up],
-                    i,
-                    j + 1,
-                )
-
-            @pl.when(j > p_down)
-            def _():
-                @pl.when(j < m - 1)
-                def _():
-                    landed(gu_high.at[t, p_down], gu_high_recv.at[t, p_down])
-                    gu[t, rows_down] = (
-                        gu[t, rows_down].astype(jnp.float32)
-                        + gu_high[t, p_down].astype(jnp.float32)
-                    ).astype(jnp.bfloat16)
-
-                send(
-                    gu.at[t, rows_down],
-                    gu_high.at[t, p_down],
-                    gu_send.at[t, p_down],
-                    gu_high_recv.at[t, p_down],
-                    i,
-                    j - 1,
-                )
-
-    own = pl.ds(pl.multiple_of(j * mine, mine), mine)
-    square = squares[own, :1]
-    for d in range(1, m):
-        p = lax.rem(j + d, m)
-        landed(squares_all.at[p], sq_recv.at[p])
-        square = square + squares_all[p, :, :1]
-    scale = lax.rsqrt(square / (m * nb * width) + 1e-06)
-    for t in range(tiles):
+                    @pl.when(come > 0)
+                    def _():
+                        landed(gu_in.at[way, t, p], gu_recv.at[way, t, p])
+                        gu[t, p] = (
+                            gu[t, p].astype(jnp.float32) + gu_in[way, t, p].astype(jnp.float32)
+                        ).astype(jnp.bfloat16)
+
+                    send(
+                        gu.at[t, p],
+                        gu_in.at[way, t, p],
+                        gu_send.at[t, p],
+                        gu_recv.at[way, t, p],
+                        i,
+                        j + ahead,
+                    )
+
+    def row_scale():
+        square = squares[pl.ds(pl.multiple_of(j * mine, mine), mine), :1]
+        for d in range(1, m):
+            p = lax.rem(j + d, m)
+            landed(squares_all.at[p], sq_recv.at[p])
+            square = square + squares_all[p, :, :1]
+        return lax.rsqrt(square / (m * nb * width) + 1e-06)
+
+    def own_hidden(t, scale):
         @pl.when(j > 0)
         def _():
-            landed(gu_low.at[t, j], gu_low_recv.at[t, j])
-            gu[t, own] = (
-                gu[t, own].astype(jnp.float32) + gu_low[t, j].astype(jnp.float32)
-            ).astype(jnp.bfloat16)
+            landed(gu_in.at[0, t, j], gu_recv.at[0, t, j])
 
         @pl.when(j < m - 1)
         def _():
-            landed(gu_high.at[t, j], gu_high_recv.at[t, j])
-            gu[t, own] = (
-                gu[t, own].astype(jnp.float32) + gu_high[t, j].astype(jnp.float32)
-            ).astype(jnp.bfloat16)
-
-        gate = gu[t, own, :tile].astype(jnp.float32) * scale
-        up = gu[t, own, tile:].astype(jnp.float32) * scale
+            landed(gu_in.at[1, t, j], gu_recv.at[1, t, j])
+
+        total = gu[t, j].astype(jnp.float32) + (
+            gu_in[0, t, j].astype(jnp.float32) + gu_in[1, t, j].astype(jnp.float32)
+        )
+        gate, up = total[:, :tile] * scale, total[:, tile:] * scale
         hidden[t, j] = (gate / (1.0 + jnp.exp(-gate)) * up).astype(jnp.bfloat16)
-
         view = hidden.at[t, j]
 
         @pl.when(j < m - 1)
@@ -429,8 +414,8 @@
         def _():
             send(view, view, hid_send_down.at[t, j], hid_recv.at[t, j], i, j - 1)
 
-    for s in range(1, m):
-        for t in range(tiles):
+    def pass_hidden(t):
+        for s in range(1, m):
             @pl.when(j >= s)
             def _():
                 view = hidden.at[t, j - s]
@@ -448,6 +433,17 @@
                 @pl.when(j > 0)
                 def _():
                     send(view, view, hid_send_down.at[t, j + s], hid_recv.at[t, j + s], i, j - 1)
+
+    for t in range(tiles + 2):
+        if t < tiles:
+            gate_up(t)
+            pass_sums(t)
+        if t == 0:
+            scale = row_scale()
+        if 1 <= t <= tiles:
+            own_hidden(t - 1, scale)
+        if t >= 2:
+            pass_hidden(t - 2)
 
     loads[3].wait()
     total = f32_dot(hidden[0].reshape(rows, tile), wd[:tile, :])
@@ -482,12 +478,12 @@
     for h in range(2):
         for step in range(chips):
             if step < chips - 1:
-                sent(att.at[h], ag_ring_send.at[h, step])
-            sent(att.at[h], ag_pair_send.at[h, step])
+                sent(gathered.at[h, 0], ag_ring_send.at[h, step])
+            sent(gathered.at[h, 0], ag_pair_send.at[h, step])
     for b in range(nb):
         @pl.when(j * nb + b != i)
         def _():
-            sent(res.at[b], res_send.at[b])
+            sent(res_all.at[0], res_send.at[b])
     for q in range(quarters):
         @pl.when(j != target)
         def _():
@@ -509,7 +505,7 @@
         for p in range(m):
             @pl.when(p != j)
             def _():
-                sent(gu_low.at[t, p], gu_send.at[t, p])
+                sent(gu.at[t, p], gu_send.at[t, p])
 
             @pl.when(jnp.logical_and(p <= j, j < m - 1))
             def _():
@@ -528,8 +524,8 @@
 
 def rest(att, res, gain, pack, unpack, wo, wg, wu, wd):
     n, m = lax.axis_size("dp"), lax.axis_size("hd")
-    _, slots, half_f = att.shape
-    nb, _, width = res.shape
+    slots, half_f = att.shape[0], att.shape[1] // 2
+    nb, width = n // m, wo.shape[1]
     rows = pack.shape[0]
     features = wd.shape[1]
     units = wd.shape[0]
@@ -549,7 +545,7 @@
         pltpu.VMEM(wu.shape, bf),
         pltpu.VMEM(wd.shape, bf),
         pltpu.VMEM((2, n, slots, half_f), bf),
-        pltpu.VMEM((2, rows, half_f), bf),
+        pltpu.VMEM((n * slots, width), f32),
         pltpu.VMEM((n, slots, width), bf),
         pltpu.VMEM((rows, width), bf),
         pltpu.VMEM((quarters, step_rows, width), bf),
@@ -558,9 +554,8 @@
         pltpu.VMEM((nb, rows, width), bf),
         pltpu.VMEM((rows, 128), f32),
         pltpu.VMEM((m, mine, 128), f32),
-        pltpu.VMEM((tiles, rows, 2 * tile), bf),
         pltpu.VMEM((tiles, m, mine, 2 * tile), bf),
-        pltpu.VMEM((tiles, m, mine, 2 * tile), bf),
+        pltpu.VMEM((2, tiles, m, mine, 2 * tile), bf),
         pltpu.VMEM((tiles, m, mine, tile), bf),
         pltpu.VMEM((rows, features), bf),
         pltpu.VMEM((chips, slots, features), bf),
@@ -583,8 +578,7 @@
         dma((m,)),
         dma((m,)),
         dma((tiles, m)),
-        dma((tiles, m)),
-        dma((tiles, m)),
+        dma((2, tiles, m)),
         dma((tiles, m)),
         dma((tiles, m)),
         dma((tiles, m)),
@@ -630,9 +624,10 @@
     n, m = lax.axis_size("dp"), lax.axis_size("hd")
     nb = n // m
     attended = attend(query_nope, query_rope, latent, key_rope, key_up, value_up, request_ids[0])
-    att = attended.reshape(slots, 2, -1).transpose(1, 0, 2)
-    res = residual.reshape(slots, nb, -1).transpose(1, 0, 2)
-    gain = norm_gain.reshape(nb, 1, -1)
+    res = residual
+    if output_weight.shape[1] % 128 != 0:
+        res = residual.reshape(slots, nb, -1).transpose(1, 0, 2)
+    gain = norm_gain.reshape(1, -1)
     rows = n * slots // 2
     first = jnp.cumsum(rank_tokens) - rank_tokens
     slot = jnp.arange(slots, dtype=jnp.int32)
@@ -643,7 +638,7 @@
     pack = (row[:, None] == packed_row.reshape(1, -1)).astype(jnp.bfloat16)
     unpack = (packed_row[:, :, None] == row[None, None, :]).astype(jnp.bfloat16)
     return rest(
-        att, res, gain, pack, unpack, output_weight, gate_weight, up_weight, down_weight
+        attended, res, gain, pack, unpack, output_weight, gate_weight, up_weight, down_weight
     )
 
 

time: 188 us -> 178 us (0.947)
  Pallas kernels: 173 us -> 164 us
    pallas_call x1, Pallas kernels: 173 us -> 164 us  [rest(): pl.pallas_call(functools.partial(layer_kernel, n, m), out_shape=jax.Shape...]
where the time goes in v2:
time: 178 us; the launch traced here: 177 us
  Pallas kernels  164 us (92%)
  matrix products  6.27 us (4%)
  local copies, waits for them, and re-layouts  4.78 us (3%)
  other arithmetic  2.21 us (1%)
    pallas_call x1, Pallas kernels, rest(): pl.pallas_call(functools.partial(layer_kernel, n, m), out_shape=jax.Shape...  164 us

profile of v2, /device:TPU:0, one launch (start us, length us, event | category | flops | bytes accessed | tf_op | source)
XLA Modules:
  0.0 177.3 jit_solution(12671452686756698627)
XLA Ops:
  0.0 0.0 copy-start
  0.0 0.0 copy-start.4
  0.0 1.5 reshape.165
  1.5 1.4 convolution_bitcast_fusion
  2.9 0.0 copy-start.1
  2.9 0.0 copy-start.2
  2.9 3.2 %fusion.7 = bf16[8,32,8,128]{3,2,1,0:T(8,128)(2,1)S(1)} fusion(bf16[64,512]{1,0:T(8,128)(2,1)} %param.16, bf16[512,4096]{1,0:T(8,128)(2,1)} %param.18), kind=kOutput, calls=%fused_computation.12 | convolution fusion | flops 268697600 | bytes 4784128 | tf_op jit(solution)/shard_map/dot_general | solution.py:19
  6.1 0.0 copy-done.4
  6.2 0.1 fusion.19
  6.2 0.0 copy-done
  6.2 0.4 fusion.5
  6.7 0.3 fusion.22
  6.9 0.0 copy-done.1
  6.9 0.0 copy-done.2
  6.9 0.8 fusion.6
  7.8 0.0 copy-start.5
  7.8 0.0 copy-start.3
  7.8 0.5 fusion.8
  8.3 0.9 copy.41
  9.2 0.0 copy-done.5
  9.2 0.2 reduce-window.9
  9.4 0.1 add_select_fusion
  9.4 0.1 select_n.21
  9.5 0.8 fusion.17.pack
  10.3 0.8 fusion.18.unpack
  11.1 0.0 copy-done.3
  11.1 0.6 reshape.167.gain
  11.7 163.9 %shard_map.136 = bf16[64,1792]{1,0:T(8,128)(2,1)} custom-call(bf16[64,4096]{1,0:T(8,128)(2,1)} %bitcast.46, bf16[64,1792]{1,0:T(8,128)(2,1)} %res.1, f32[1,1792]{1,0:T(1,128)} %reshape.167.gain, bf16[256,512]{1,0:T(8,128)(2,1)} %fusion.17.pack, bf16[8,64,256]{2,1,0:T(8,128)(2,1)} %fusion.18.unpack, bf16[4096,896]{1,0:T(8,128)(2,1)} %wo_hbm.1, ...), custom_call_target="tpu_custom_call" | custom-call | flops 8220835840 | bytes 32112640 | tf_op jit(solution)/shard_map/pallas_call | solution.py:590
  175.6 1.6 copy.43
  (1 shorter events, 0.0 us)
Async XLA Ops:
  0.0 6.2 %copy-start = (bf16[64,4096]{1,0:T(8,128)(2,1)S(1)}, bf16[64,4096]{1,0:T(8,128)(2,1)}, u32[]{:S(2)}) copy-start(bf16[64,4096]{1,0:T(8,128)(2,1)} %param.14) | copy-start | bytes 1572868
  0.0 6.1 %copy-start.4 = (s32[1,64]{1,0:T(1,128)S(1)}, s32[1,64]{1,0:T(1,128)}, u32[]{:S(2)}) copy-start(s32[1,64]{1,0:T(1,128)} %param.27) | copy-start | bytes 772
  2.9 4.0 %copy-start.1 = (bf16[512,4096]{1,0:T(8,128)(2,1)S(1)}, bf16[512,4096]{1,0:T(8,128)(2,1)}, u32[]{:S(2)}) copy-start(bf16[512,4096]{1,0:T(8,128)(2,1)} %param.19) | copy-start | bytes 12582916
  2.9 4.0 %copy-start.2 = (bf16[64,512]{1,0:T(8,128)(2,1)S(1)}, bf16[64,512]{1,0:T(8,128)(2,1)}, u32[]{:S(2)}) copy-start(bf16[64,512]{1,0:T(8,128)(2,1)} %param.16) | copy-start | bytes 196612
  7.8 1.4 copy-start.5
  7.8 3.3 %copy-start.3 = (f32[1792]{0:T(1024)S(1)}, f32[1792]{0:T(1024)}, u32[]{:S(2)}) copy-start(f32[1792]{0:T(1024)} %param.22) | copy-start | bytes 21508

commit v3 on v2

--- a/solution.py
+++ b/solution.py
@@ -81,6 +81,7 @@
     gu,
     gu_in,
     hidden,
+    mlp,
     y,
     y_pair,
     pair_in,
@@ -103,8 +104,7 @@
     sq_recv,
     gu_send,
     gu_recv,
-    hid_send_up,
-    hid_send_down,
+    hid_send,
     hid_recv,
     pair_send,
     pair_recv,
@@ -121,10 +121,11 @@
     nb, rows, width = mixed.shape
     tiles = gu.shape[0]
     tile = gu.shape[3] // 2
-    mine = rows // m
+    mine = rows // 2
     quarters = from_low.shape[0]
     step_rows = rows // quarters
-    half_f = gathered.shape[3]
+    parts, half_f = gathered.shape[0], gathered.shape[3]
+    turns = [h for p in range(parts // 2) for h in (p, p + parts // 2)]
     slots = att.shape[0]
 
     def att_half(h):
@@ -179,24 +180,24 @@
         )
     pl.semaphore_wait(barrier, n + m - 2)
 
-    for h in range(2):
+    for h in turns:
         send(
             att_half(h),
             gathered.at[h, i],
             ag_ring_send.at[h, 0],
             ag_recv.at[h, i],
-            (after, before)[h],
+            (after, before)[h // (parts // 2)],
             j,
         )
-    for h in range(2):
+    for h in turns:
         send(att_half(h), gathered.at[h, i], ag_pair_send.at[h, 0], ag_recv.at[h, i], sibling, j)
         pltpu.make_async_copy(att_half(h), gathered.at[h, i], own_sem.at[h]).start()
     loads[0].wait()
     for load in loads[1:]:
         load.start()
     for step in range(chips):
-        sources = [chip_at(here - step), chip_at(here + step)]
-        for h in range(2):
+        sources = [chip_at(here - step if h < parts // 2 else here + step) for h in range(parts)]
+        for h in turns:
             block = 2 * sources[h] + core
             if step == 0:
                 pltpu.make_async_copy(att_half(h), gathered.at[h, i], own_sem.at[h]).wait()
@@ -209,7 +210,7 @@
                     view,
                     ag_ring_send.at[h, step],
                     ag_recv.at[h, block],
-                    (after, before)[h],
+                    (after, before)[h // (parts // 2)],
                     j,
                 )
             send(view, view, ag_pair_send.at[h, step], ag_recv.at[h, block], sibling, j)
@@ -225,14 +226,14 @@
                 def _():
                     pltpu.make_async_copy(res_block(b), res_all.at[i], res_send.at[b]).start()
 
-        for h in range(2):
+        for h in turns:
             block = 2 * sources[h] + 1 - core
             landed(gathered.at[h, block], ag_recv.at[h, block])
             both = gathered[h, pl.ds(2 * sources[h], 2)].reshape(2 * slots, half_f)
             sl = pl.ds(pl.multiple_of(2 * sources[h] * slots, 2 * slots), 2 * slots)
             term = f32_dot(both, wo[h * half_f : (h + 1) * half_f, :])
-            first = step == 0 and h == 0 or step > 0 and 2 * step < chips
-            first = first or (2 * step == chips and h == 0)
+            opens = [0] if step == 0 or 2 * step == chips else [0, parts // 2]
+            first = h in opens and 2 * step <= chips
             acc[sl] = term if first else acc[sl] + term
     part[...] = f32_dot(pack[...], acc[...].astype(jnp.bfloat16)).astype(jnp.bfloat16)
 
@@ -324,27 +325,21 @@
         scaled[b] = (wide * gain[:, b * width : (b + 1) * width]).astype(jnp.bfloat16)
         total = total + jnp.sum(wide * wide, axis=1, keepdims=True)
     squares[...] = jnp.broadcast_to(total, squares.shape)
-    for d in range(1, m):
-        p = lax.rem(j + d, m)
-        send(
-            squares.at[pl.ds(p * mine, mine)],
-            squares_all.at[j],
-            sq_send.at[d],
-            sq_recv.at[j],
-            i,
-            p,
-        )
+    ends = (0, m - 1)
+    for e in range(2):
+        @pl.when(j != ends[e])
+        def _():
+            send(
+                squares.at[pl.ds(e * mine, mine)],
+                squares_all.at[j],
+                sq_send.at[e],
+                sq_recv.at[j],
+                i,
+                ends[e],
+            )
+
     loads[1].wait()
     loads[2].wait()
-    for t in range(tiles):
-        @pl.when(j == 0)
-        def _():
-            gu_in[0, t, 0] = jnp.zeros_like(gu_in[0, t, 0])
-
-        @pl.when(j == m - 1)
-        def _():
-            gu_in[1, t, m - 1] = jnp.zeros_like(gu_in[1, t, m - 1])
-
     def gate_up(t):
         cols = slice(t * tile, (t + 1) * tile)
         gate = f32_dot(scaled[0], wg[:width, cols])
@@ -352,103 +347,91 @@
         for b in range(1, nb):
             gate = gate + f32_dot(scaled[b], wg[b * width : (b + 1) * width, cols])
             up = up + f32_dot(scaled[b], wu[b * width : (b + 1) * width, cols])
-        gu[t, :, :, :tile] = gate.astype(jnp.bfloat16).reshape(m, mine, tile)
-        gu[t, :, :, tile:] = up.astype(jnp.bfloat16).reshape(m, mine, tile)
+        gu[t, :, :, :tile] = gate.astype(jnp.bfloat16).reshape(2, mine, tile)
+        gu[t, :, :, tile:] = up.astype(jnp.bfloat16).reshape(2, mine, tile)
 
     def pass_sums(t):
-        for s in range(m - 1):
-            for turn in range(2):
-                nearer = (2 * j) // m
-                way = nearer if turn == 0 else 1 - nearer
-                p = (1 - way) * (m - 1 - s) + way * s
-                ahead = 1 - 2 * way
-                come = (1 - way) * j + way * (m - 1 - j)
-
-                @pl.when((p - j) * ahead > 0)
+        for turn in range(2):
+            nearer = (2 * j) // m
+            e = 1 - nearer if turn == 0 else nearer
+            come = e * j + (1 - e) * (m - 1 - j)
+
+            @pl.when(come < m - 1)
+            def _():
+                @pl.when(come > 0)
                 def _():
-                    @pl.when(come > 0)
-                    def _():
-                        landed(gu_in.at[way, t, p], gu_recv.at[way, t, p])
-                        gu[t, p] = (
-                            gu[t, p].astype(jnp.float32) + gu_in[way, t, p].astype(jnp.float32)
-                        ).astype(jnp.bfloat16)
-
+                    landed(gu_in.at[e, t], gu_recv.at[t, e])
+                    gu[t, e] = (
+                        gu[t, e].astype(jnp.float32) + gu_in[e, t].astype(jnp.float32)
+                    ).astype(jnp.bfloat16)
+
+                send(
+                    gu.at[t, e], gu_in.at[e, t], gu_send.at[t, e], gu_recv.at[t, e], i, j + 2 * e - 1
+                )
+
+    for t in range(tiles):
+        gate_up(t)
+        pass_sums(t)
+
+    def hidden_tile(e, t):
+        return hidden.at[e, :, pl.ds(t * tile, tile)]
+
+    for e in range(2):
+        @pl.when(j == ends[e])
+        def _():
+            square = squares[e * mine : (e + 1) * mine, :1]
+            for p in range(m):
+                if p != ends[e]:
+                    landed(squares_all.at[p], sq_recv.at[p])
+                    square = square + squares_all[p, :, :1]
+            scale = lax.rsqrt(square / (m * nb * width) + 1e-06)
+            for t in range(tiles):
+                landed(gu_in.at[e, t], gu_recv.at[t, e])
+                total = gu[t, e].astype(jnp.float32) + gu_in[e, t].astype(jnp.float32)
+                gate, up = total[:, :tile] * scale, total[:, tile:] * scale
+                hidden[e, :, t * tile : (t + 1) * tile] = (
+                    gate / (1.0 + jnp.exp(-gate)) * up
+                ).astype(jnp.bfloat16)
+                send(
+                    hidden_tile(e, t),
+                    hidden_tile(e, t),
+                    hid_send.at[t, e],
+                    hid_recv.at[t, e],
+                    i,
+                    j + 1 - 2 * e,
+                )
+
+    loads[3].wait()
+    group = 3 if tiles % 3 == 0 else 1
+    for t in range(tiles):
+        for turn in range(2):
+            nearer = (2 * j) // m
+            e = nearer if turn == 0 else 1 - nearer
+            gone = (1 - e) * j + e * (m - 1 - j)
+
+            @pl.when(gone > 0)
+            def _():
+                landed(hidden_tile(e, t), hid_recv.at[t, e])
+
+                @pl.when(gone < m - 1)
+                def _():
                     send(
-                        gu.at[t, p],
-                        gu_in.at[way, t, p],
-                        gu_send.at[t, p],
-                        gu_recv.at[way, t, p],
+                        hidden_tile(e, t),
+                        hidden_tile(e, t),
+                        hid_send.at[t, e],
+                        hid_recv.at[t, e],
                         i,
-                        j + ahead,
+                        j + 1 - 2 * e,
                     )
 
-    def row_scale():
-        square = squares[pl.ds(pl.multiple_of(j * mine, mine), mine), :1]
-        for d in range(1, m):
-            p = lax.rem(j + d, m)
-            landed(squares_all.at[p], sq_recv.at[p])
-            square = square + squares_all[p, :, :1]
-        return lax.rsqrt(square / (m * nb * width) + 1e-06)
-
-    def own_hidden(t, scale):
-        @pl.when(j > 0)
-        def _():
-            landed(gu_in.at[0, t, j], gu_recv.at[0, t, j])
-
-        @pl.when(j < m - 1)
-        def _():
-            landed(gu_in.at[1, t, j], gu_recv.at[1, t, j])
-
-        total = gu[t, j].astype(jnp.float32) + (
-            gu_in[0, t, j].astype(jnp.float32) + gu_in[1, t, j].astype(jnp.float32)
-        )
-        gate, up = total[:, :tile] * scale, total[:, tile:] * scale
-        hidden[t, j] = (gate / (1.0 + jnp.exp(-gate)) * up).astype(jnp.bfloat16)
-        view = hidden.at[t, j]
-
-        @pl.when(j < m - 1)
-        def _():
-            send(view, view, hid_send_up.at[t, j], hid_recv.at[t, j], i, j + 1)
-
-        @pl.when(j > 0)
-        def _():
-            send(view, view, hid_send_down.at[t, j], hid_recv.at[t, j], i, j - 1)
-
-    def pass_hidden(t):
-        for s in range(1, m):
-            @pl.when(j >= s)
-            def _():
-                view = hidden.at[t, j - s]
-                landed(view, hid_recv.at[t, j - s])
-
-                @pl.when(j < m - 1)
-                def _():
-                    send(view, view, hid_send_up.at[t, j - s], hid_recv.at[t, j - s], i, j + 1)
-
-            @pl.when(j + s <= m - 1)
-            def _():
-                view = hidden.at[t, j + s]
-                landed(view, hid_recv.at[t, j + s])
-
-                @pl.when(j > 0)
-                def _():
-                    send(view, view, hid_send_down.at[t, j + s], hid_recv.at[t, j + s], i, j - 1)
-
-    for t in range(tiles + 2):
-        if t < tiles:
-            gate_up(t)
-            pass_sums(t)
-        if t == 0:
-            scale = row_scale()
-        if 1 <= t <= tiles:
-            own_hidden(t - 1, scale)
-        if t >= 2:
-            pass_hidden(t - 2)
-
-    loads[3].wait()
-    total = f32_dot(hidden[0].reshape(rows, tile), wd[:tile, :])
-    for t in range(1, tiles):
-        total = total + f32_dot(hidden[t].reshape(rows, tile), wd[t * tile : (t + 1) * tile, :])
+        if t % group == group - 1:
+            units = slice((t + 1 - group) * tile, (t + 1) * tile)
+            term = f32_dot(hidden[:, :, units].reshape(rows, group * tile), wd[units, :])
+            if t >= group:
+                term = mlp[...] + term
+            if t < tiles - 1:
+                mlp[...] = term
+    total = term
     y[...] = total.astype(jnp.bfloat16)
 
     for d in range(chips):
@@ -475,7 +458,7 @@
     def sent(ref, sem):
         pltpu.make_async_copy(ref, ref, sem).wait()
 
-    for h in range(2):
+    for h in range(parts):
         for step in range(chips):
             if step < chips - 1:
                 sent(gathered.at[h, 0], ag_ring_send.at[h, step])
@@ -499,21 +482,20 @@
                 sent(from_low.at[q], bc_ring_send.at[bb, q])
 
             sent(from_low.at[q], bc_pair_send.at[bb, q])
-    for d in range(1, m):
-        sent(squares_all.at[0], sq_send.at[d])
-    for t in range(tiles):
-        for p in range(m):
-            @pl.when(p != j)
+    for e in range(2):
+        @pl.when(j != ends[e])
+        def _():
+            sent(squares_all.at[0], sq_send.at[e])
+
+        for t in range(tiles):
+            @pl.when(j != ends[e])
             def _():
-                sent(gu.at[t, p], gu_send.at[t, p])
-
-            @pl.when(jnp.logical_and(p <= j, j < m - 1))
+                sent(gu.at[t, e], gu_send.at[t, e])
+
+            @pl.when(j != ends[1 - e])
             def _():
-                sent(hidden.at[t, p], hid_send_up.at[t, p])
-
-            @pl.when(jnp.logical_and(p >= j, j > 0))
-            def _():
-                sent(hidden.at[t, p], hid_send_down.at[t, p])
+                sent(hidden_tile(e, t), hid_send.at[t, e])
+
     for c in range(chips):
         sent(y_pair.at[c], pair_send.at[c])
 
@@ -524,16 +506,17 @@
 
 def rest(att, res, gain, pack, unpack, wo, wg, wu, wd):
     n, m = lax.axis_size("dp"), lax.axis_size("hd")
-    slots, half_f = att.shape[0], att.shape[1] // 2
+    parts = 4
+    slots, half_f = att.shape[0], att.shape[1] // parts
     nb, width = n // m, wo.shape[1]
     rows = pack.shape[0]
     features = wd.shape[1]
     units = wd.shape[0]
-    tiles = 3 if units % 384 == 0 else 1
+    tiles = units // 256 if units % 256 == 0 else 1
     tile = units // tiles
-    quarters = 4
+    quarters = 8
     chips = n // 2
-    mine = rows // m
+    mine = rows // 2
     bf, f32 = jnp.bfloat16, jnp.float32
     vmem = pl.BlockSpec(memory_space=pltpu.VMEM)
     hbm = pl.BlockSpec(memory_space=pl.ANY)
@@ -544,7 +527,7 @@
         pltpu.VMEM(wg.shape, bf),
         pltpu.VMEM(wu.shape, bf),
         pltpu.VMEM(wd.shape, bf),
-        pltpu.VMEM((2, n, slots, half_f), bf),
+        pltpu.VMEM((parts, n, slots, half_f), bf),
         pltpu.VMEM((n * slots, width), f32),
         pltpu.VMEM((n, slots, width), bf),
         pltpu.VMEM((rows, width), bf),
@@ -554,19 +537,20 @@
         pltpu.VMEM((nb, rows, width), bf),
         pltpu.VMEM((rows, 128), f32),
         pltpu.VMEM((m, mine, 128), f32),
-        pltpu.VMEM((tiles, m, mine, 2 * tile), bf),
-        pltpu.VMEM((2, tiles, m, mine, 2 * tile), bf),
-        pltpu.VMEM((tiles, m, mine, tile), bf),
+        pltpu.VMEM((tiles, 2, mine, 2 * tile), bf),
+        pltpu.VMEM((2, tiles, mine, 2 * tile), bf),
+        pltpu.VMEM((2, mine, units), bf),
+        pltpu.VMEM((rows, features), f32),
         pltpu.VMEM((rows, features), bf),
         pltpu.VMEM((chips, slots, features), bf),
         pltpu.VMEM((chips, slots, features), bf),
         pltpu.VMEM((chips, slots, features), bf),
         pltpu.VMEM((chips, slots, features), bf),
         dma((4,)),
-        dma((2,)),
-        dma((2, chips)),
-        dma((2, chips)),
-        dma((2, n)),
+        dma((parts,)),
+        dma((parts, chips)),
+        dma((parts, chips)),
+        dma((parts, n)),
         dma((nb,)),
         dma((n,)),
         dma((quarters,)),
@@ -577,11 +561,10 @@
         dma((nb, quarters)),
         dma((m,)),
         dma((m,)),
-        dma((tiles, m)),
-        dma((2, tiles, m)),
-        dma((tiles, m)),
-        dma((tiles, m)),
-        dma((tiles, m)),
+        dma((tiles, 2)),
+        dma((tiles, 2)),
+        dma((tiles, 2)),
+        dma((tiles, 2)),
         dma((chips,)),
         dma((chips,)),
         dma((chips,)),

time: 178 us -> 215 us (1.21)
  Pallas kernels: 164 us -> 201 us
    pallas_call x1, Pallas kernels: 164 us -> 201 us  [rest(): pl.pallas_call(functools.partial(layer_kernel, n, m), out_shape=jax.Shape...]
where the time goes in v3:
time: 215 us; the launch traced here: 214 us
  Pallas kernels  201 us (93%)
  matrix products  6.27 us (3%)
  local copies, waits for them, and re-layouts  4.78 us (2%)
  other arithmetic  2.21 us (1%)
    pallas_call x1, Pallas kernels, rest(): pl.pallas_call(functools.partial(layer_kernel, n, m), out_shape=jax.Shape...  201 us

profile of v3, /device:TPU:0, one launch (start us, length us, event | category | flops | bytes accessed | tf_op | source)
XLA Modules:
  0.0 214.4 jit_solution(11667828620152624162)
XLA Ops:
  0.0 0.0 copy-start
  0.0 0.0 copy-start.4
  0.0 1.5 reshape.165
  1.5 1.4 convolution_bitcast_fusion
  2.9 0.0 copy-start.1
  2.9 0.0 copy-start.2
  2.9 3.2 %fusion.7 = bf16[8,32,8,128]{3,2,1,0:T(8,128)(2,1)S(1)} fusion(bf16[64,512]{1,0:T(8,128)(2,1)} %param.16, bf16[512,4096]{1,0:T(8,128)(2,1)} %param.18), kind=kOutput, calls=%fused_computation.12 | convolution fusion | flops 268697600 | bytes 4784128 | tf_op jit(solution)/shard_map/dot_general | solution.py:19
  6.1 0.0 copy-done.4
  6.2 0.1 fusion.19
  6.2 0.0 copy-done
  6.2 0.4 fusion.5
  6.7 0.3 fusion.22
  6.9 0.0 copy-done.1
  6.9 0.0 copy-done.2
  6.9 0.8 fusion.6
  7.8 0.0 copy-start.5
  7.8 0.0 copy-start.3
  7.8 0.5 fusion.8
  8.3 0.9 copy.41
  9.2 0.0 copy-done.5
  9.2 0.2 reduce-window.9
  9.4 0.1 add_select_fusion
  9.4 0.1 select_n.21
  9.5 0.8 fusion.17.pack
  10.3 0.8 fusion.18.unpack
  11.1 0.0 copy-done.3
  11.1 0.6 reshape.167.gain
  11.7 201.0 %shard_map.136 = bf16[64,1792]{1,0:T(8,128)(2,1)} custom-call(bf16[64,4096]{1,0:T(8,128)(2,1)} %bitcast.46, bf16[64,1792]{1,0:T(8,128)(2,1)} %res.1, f32[1,1792]{1,0:T(1,128)} %reshape.167.gain, bf16[256,512]{1,0:T(8,128)(2,1)} %fusion.17.pack, bf16[8,64,256]{2,1,0:T(8,128)(2,1)} %fusion.18.unpack, bf16[4096,896]{1,0:T(8,128)(2,1)} %wo_hbm.1, ...), custom_call_target="tpu_custom_call" | custom-call | flops 8220835840 | bytes 32112640 | tf_op jit(solution)/shard_map/pallas_call | solution.py:573
  212.8 1.6 copy.43
  (1 shorter events, 0.0 us)
Async XLA Ops:
  0.0 6.2 %copy-start = (bf16[64,4096]{1,0:T(8,128)(2,1)S(1)}, bf16[64,4096]{1,0:T(8,128)(2,1)}, u32[]{:S(2)}) copy-start(bf16[64,4096]{1,0:T(8,128)(2,1)} %param.14) | copy-start | bytes 1572868
  0.0 6.1 %copy-start.4 = (s32[1,64]{1,0:T(1,128)S(1)}, s32[1,64]{1,0:T(1,128)}, u32[]{:S(2)}) copy-start(s32[1,64]{1,0:T(1,128)} %param.27) | copy-start | bytes 772
  2.9 4.0 %copy-start.1 = (bf16[512,4096]{1,0:T(8,128)(2,1)S(1)}, bf16[512,4096]{1,0:T(8,128)(2,1)}, u32[]{:S(2)}) copy-start(bf16[512,4096]{1,0:T(8,128)(2,1)} %param.19) | copy-start | bytes 12582916
  2.9 4.0 %copy-start.2 = (bf16[64,512]{1,0:T(8,128)(2,1)S(1)}, bf16[64,512]{1,0:T(8,128)(2,1)}, u32[]{:S(2)}) copy-start(bf16[64,512]{1,0:T(8,128)(2,1)} %param.16) | copy-start | bytes 196612
  7.8 1.4 copy-start.5
  7.8 3.3 %copy-start.3 = (f32[1792]{0:T(1024)S(1)}, f32[1792]{0:T(1024)}, u32[]{:S(2)}) copy-start(f32[1792]{0:T(1024)} %param.22) | copy-start | bytes 21508

commit v4 on v3

--- a/solution.py
+++ b/solution.py
@@ -240,14 +240,20 @@
     target = i // nb
     slot = lax.rem(i, nb)
 
-    def bc_forward(b, q, source_chip):
-        up = q < quarters // 2
-        far = lax.rem((here - place(source_chip) if up else place(source_chip) - here) + chips, chips)
-
-        @pl.when(far < chips - 1)
-        def _():
-            sl = mixed.at[b, pl.ds(q * step_rows, step_rows)]
-            send(sl, sl, bc_ring_send.at[b // 2, q], bc_recv.at[b, q], after if up else before, j)
+    def ring_far(way, source_chip):
+        up = here - place(source_chip)
+        return lax.rem((1 - 2 * way) * up + chips, chips)
+
+    def row_chunk(q):
+        return pl.ds(pl.multiple_of(q * step_rows, step_rows), step_rows)
+
+    def bc_forward(b, q, way, source_chip):
+        onward = (1 - way) * after + way * before
+
+        @pl.when(ring_far(way, source_chip) < chips - 1)
+        def _():
+            view = mixed.at[b, row_chunk(q)]
+            send(view, view, bc_ring_send.at[b // 2, q], bc_recv.at[b, q], onward, j)
 
     @pl.when(j == target)
     def _():
@@ -296,22 +302,29 @@
             total = mixed[slot, sl].astype(jnp.float32) + part[sl].astype(jnp.float32)
             total = total + (from_low[q].astype(jnp.float32) + from_high[q].astype(jnp.float32))
             mixed[slot, sl] = total.astype(jnp.bfloat16)
-            bc_forward(slot, q, chip)
+            bc_forward(slot, q, q // (quarters // 2), chip)
             view = mixed.at[slot, sl]
             send(view, view, bc_pair_send.at[slot // 2, q], bc_recv.at[slot, q], sibling, j)
 
-    for q in [x for p in range(quarters // 2) for x in (p, p + quarters // 2)]:
-        sl = pl.ds(q * step_rows, step_rows)
+    lag = 2
+    for x in range(quarters // 2 + lag):
         for bb in range(nb // 2):
             b = 2 * bb + core
             source = (j * nb + b) // 2
-
-            @pl.when(source != chip)
-            def _():
-                view = mixed.at[b, sl]
-                landed(view, bc_recv.at[b, q])
-                bc_forward(b, q, source)
-                send(view, view, bc_pair_send.at[bb, q], bc_recv.at[b, q], sibling, j)
+            nearer = (2 * ring_far(0, source)) // (chips + 1)
+            for turn in range(2):
+                p = x - lag * turn
+                if not 0 <= p < quarters // 2:
+                    continue
+                way = nearer if turn == 0 else 1 - nearer
+                q = way * (quarters // 2) + p
+
+                @pl.when(source != chip)
+                def _():
+                    view = mixed.at[b, row_chunk(q)]
+                    landed(view, bc_recv.at[b, q])
+                    bc_forward(b, q, way, source)
+                    send(view, view, bc_pair_send.at[bb, q], bc_recv.at[b, q], sibling, j)
 
     for q in range(quarters):
         sl = pl.ds(q * step_rows, step_rows)
@@ -350,28 +363,28 @@
         gu[t, :, :, :tile] = gate.astype(jnp.bfloat16).reshape(2, mine, tile)
         gu[t, :, :, tile:] = up.astype(jnp.bfloat16).reshape(2, mine, tile)
 
-    def pass_sums(t):
-        for turn in range(2):
-            nearer = (2 * j) // m
-            e = 1 - nearer if turn == 0 else nearer
-            come = e * j + (1 - e) * (m - 1 - j)
-
-            @pl.when(come < m - 1)
+    nearer = (2 * j) // m
+
+    def pass_sums(t, e):
+        come = e * j + (1 - e) * (m - 1 - j)
+
+        @pl.when(come < m - 1)
+        def _():
+            @pl.when(come > 0)
             def _():
-                @pl.when(come > 0)
-                def _():
-                    landed(gu_in.at[e, t], gu_recv.at[t, e])
-                    gu[t, e] = (
-                        gu[t, e].astype(jnp.float32) + gu_in[e, t].astype(jnp.float32)
-                    ).astype(jnp.bfloat16)
-
-                send(
-                    gu.at[t, e], gu_in.at[e, t], gu_send.at[t, e], gu_recv.at[t, e], i, j + 2 * e - 1
-                )
-
-    for t in range(tiles):
-        gate_up(t)
-        pass_sums(t)
+                landed(gu_in.at[e, t], gu_recv.at[t, e])
+                gu[t, e] = (
+                    gu[t, e].astype(jnp.float32) + gu_in[e, t].astype(jnp.float32)
+                ).astype(jnp.bfloat16)
+
+            send(gu.at[t, e], gu_in.at[e, t], gu_send.at[t, e], gu_recv.at[t, e], i, j + 2 * e - 1)
+
+    for t in range(tiles + lag):
+        if t < tiles:
+            gate_up(t)
+            pass_sums(t, 1 - nearer)
+        if t >= lag:
+            pass_sums(t - lag, nearer)
 
     def hidden_tile(e, t):
         return hidden.at[e, :, pl.ds(t * tile, tile)]
@@ -403,27 +416,31 @@
 
     loads[3].wait()
     group = 3 if tiles % 3 == 0 else 1
-    for t in range(tiles):
-        for turn in range(2):
-            nearer = (2 * j) // m
-            e = nearer if turn == 0 else 1 - nearer
-            gone = (1 - e) * j + e * (m - 1 - j)
-
-            @pl.when(gone > 0)
+    def pass_hidden(t, e):
+        gone = (1 - e) * j + e * (m - 1 - j)
+
+        @pl.when(gone > 0)
+        def _():
+            landed(hidden_tile(e, t), hid_recv.at[t, e])
+
+            @pl.when(gone < m - 1)
             def _():
-                landed(hidden_tile(e, t), hid_recv.at[t, e])
-
-                @pl.when(gone < m - 1)
-                def _():
-                    send(
-                        hidden_tile(e, t),
-                        hidden_tile(e, t),
-                        hid_send.at[t, e],
-                        hid_recv.at[t, e],
-                        i,
-                        j + 1 - 2 * e,
-                    )
-
+                send(
+                    hidden_tile(e, t),
+                    hidden_tile(e, t),
+                    hid_send.at[t, e],
+                    hid_recv.at[t, e],
+                    i,
+                    j + 1 - 2 * e,
+                )
+
+    for x in range(tiles + lag):
+        if x < tiles:
+            pass_hidden(x, nearer)
+        t = x - lag
+        if t < 0:
+            continue
+        pass_hidden(t, 1 - nearer)
         if t % group == group - 1:
             units = slice((t + 1 - group) * tile, (t + 1) * tile)
             term = f32_dot(hidden[:, :, units].reshape(rows, group * tile), wd[units, :])
@@ -474,10 +491,7 @@
 
         for bb in range(nb // 2):
             source = (j * nb + 2 * bb + core) // 2
-            up = q < quarters // 2
-            far = lax.rem((here - place(source) if up else place(source) - here) + chips, chips)
-
-            @pl.when(far < chips - 1)
+            @pl.when(ring_far(q // (quarters // 2), source) < chips - 1)
             def _():
                 sent(from_low.at[q], bc_ring_send.at[bb, q])
 

time: 215 us -> 145 us (0.67)
  Pallas kernels: 201 us -> 131 us
    pallas_call x1, Pallas kernels: 201 us -> 131 us  [rest(): pl.pallas_call(functools.partial(layer_kernel, n, m), out_shape=jax.Shape...]
where the time goes in v4:
time: 145 us
  Pallas kernels  131 us (90%)
  matrix products  6.27 us (4%)
  local copies, waits for them, and re-layouts  4.78 us (3%)
  other arithmetic  2.21 us (2%)
    pallas_call x1, Pallas kernels, rest(): pl.pallas_call(functools.partial(layer_kernel, n, m), out_shape=jax.Shape...  131 us
    dot_general x1, matrix products, attend(): jnp.dot(latent, key_up, preferred_element_type=jnp.float32)  3.21 us

profile of v4, /device:TPU:0, one launch (start us, length us, event | category | flops | bytes accessed | tf_op | source)
XLA Modules:
  0.0 144.8 jit_solution(10080517706104085688)
XLA Ops:
  0.0 0.0 copy-start
  0.0 0.0 copy-start.4
  0.0 1.5 %reshape.165 = bf16[64,32,64]{2,1,0:T(8,128)(2,1)S(1)} reshape(bf16[64,2048]{1,0:T(8,128)(2,1)} %param.15) | data formatting | bytes 524288 | tf_op jit(solution)/shard_map/reshape | solution.py:22
  1.5 1.4 convolution_bitcast_fusion
  2.9 0.0 copy-start.1
  2.9 0.0 copy-start.2
  2.9 3.2 %fusion.7 = bf16[8,32,8,128]{3,2,1,0:T(8,128)(2,1)S(1)} fusion(bf16[64,512]{1,0:T(8,128)(2,1)} %param.16, bf16[512,4096]{1,0:T(8,128)(2,1)} %param.18), kind=kOutput, calls=%fused_computation.12 | convolution fusion | flops 268697600 | bytes 4784128 | tf_op jit(solution)/shard_map/dot_general | solution.py:19
  6.1 0.0 copy-done.4
  6.2 0.1 fusion.19
  6.2 0.0 copy-done
  6.2 0.4 fusion.5
  6.7 0.3 fusion.22
  6.9 0.0 copy-done.1
  6.9 0.0 copy-done.2
  6.9 0.8 fusion.6
  7.8 0.0 copy-start.5
  7.8 0.0 copy-start.3
  7.8 0.5 fusion.8
  8.3 0.9 copy.41
  9.2 0.0 copy-done.5
  9.2 0.2 reduce-window.9
  9.4 0.1 add_select_fusion
  9.4 0.1 select_n.21
  9.5 0.8 fusion.17.pack
  10.3 0.8 fusion.18.unpack
  11.1 0.0 copy-done.3
  11.1 0.6 reshape.167.gain
  11.7 131.5 %shard_map.136 = bf16[64,1792]{1,0:T(8,128)(2,1)} custom-call(bf16[64,4096]{1,0:T(8,128)(2,1)} %bitcast.46, bf16[64,1792]{1,0:T(8,128)(2,1)} %res.1, f32[1,1792]{1,0:T(1,128)} %reshape.167.gain, bf16[256,512]{1,0:T(8,128)(2,1)} %fusion.17.pack, bf16[8,64,256]{2,1,0:T(8,128)(2,1)} %fusion.18.unpack, bf16[4096,896]{1,0:T(8,128)(2,1)} %wo_hbm.1, ...), custom_call_target="tpu_custom_call" | custom-call | flops 8220835840 | bytes 32112640 | tf_op jit(solution)/shard_map/pallas_call | solution.py:587
  143.2 1.6 %copy.43 = bf16[64,1792]{1,0:T(8,128)(2,1)} copy(bf16[64,1792]{1,0:T(8,128)(2,1)} %shard_map.136) | data formatting | bytes 458752
  (1 shorter events, 0.0 us)
Async XLA Ops:
  0.0 6.2 %copy-start = (bf16[64,4096]{1,0:T(8,128)(2,1)S(1)}, bf16[64,4096]{1,0:T(8,128)(2,1)}, u32[]{:S(2)}) copy-start(bf16[64,4096]{1,0:T(8,128)(2,1)} %param.14) | copy-start | bytes 1572868
  0.0 6.1 %copy-start.4 = (s32[1,64]{1,0:T(1,128)S(1)}, s32[1,64]{1,0:T(1,128)}, u32[]{:S(2)}) copy-start(s32[1,64]{1,0:T(1,128)} %param.27) | copy-start | bytes 772
  2.9 4.0 %copy-start.1 = (bf16[512,4096]{1,0:T(8,128)(2,1)S(1)}, bf16[512,4096]{1,0:T(8,128)(2,1)}, u32[]{:S(2)}) copy-start(bf16[512,4096]{1,0:T(8,128)(2,1)} %param.19) | copy-start | bytes 12582916
  2.9 4.0 %copy-start.2 = (bf16[64,512]{1,0:T(8,128)(2,1)S(1)}, bf16[64,512]{1,0:T(8,128)(2,1)}, u32[]{:S(2)}) copy-start(bf16[64,512]{1,0:T(8,128)(2,1)} %param.16) | copy-start | bytes 196612
  7.8 1.4 copy-start.5
  7.8 3.3 %copy-start.3 = (f32[1792]{0:T(1024)S(1)}, f32[1792]{0:T(1024)}, u32[]{:S(2)}) copy-start(f32[1792]{0:T(1024)} %param.22) | copy-start | bytes 21508
